TPU v7x, 32 devices: a whole 2x2x4 slice. The times are simulated.
32 devices in a mesh: row: 4 (over z), col: 4 (over y, x), ch: 2 (over core).
Axes of the slice: x: 2, y: 2, z: 4, core: 2. Of those that a mesh axis runs over, the one named last changes fastest.
Arguments:
- field: float32 [32, 512, 2048], P(None, 'row', 'col'), may hold values from -6 to 6
- spec_weight: float32 [2, 32, 32, 512], replicated, may hold values from -0.75 to 0.75
- point_weight: float32 [32, 32], replicated, may hold values from -1 to 1
- bias: float32 [32], P('ch'), may hold values from -1 to 1
- kept_modes: int32 [32], replicated, may hold values from 8 to 16, as said below
- residual: float32 [32, 16384], P('ch', ('row', 'col')), may hold values from -6 to 6
- trace_dest: int32 [16384, 1], P(('row', 'col')), may hold values from 0 to 15; in each aligned block of 1024 rows (0 to 1023, 1024 to 2047, ...) at most 128 rows name the same one
- trace_cell: int32 [16384], P(('row', 'col')), may hold values from 0 to 65535
Outputs:
- grad_field: float32 [32, 512, 2048], P('ch', 'row', 'col')
- grad_spec: float32 [2, 32, 32, 512], P(None, None, 'ch')
- grad_point: float32 [32, 32], P(None, 'ch')
- grad_bias: float32 [32], P('ch')
Inputs may be any that keep to these rules, and one draw needn't show every extreme that they name: `trace_dest`: of the 1024 points of one device, at most 128 go to one tile. `kept_modes`: some channel keeps 16 and some keeps 16 // 2.
All inputs are finite; a program needn't handle non-finite values.
Results may differ from a plain program's by a relative error of at most 0.00012.
Values sent between devices are 32-bit elements; how exact they have to be, the bound alone decides.
A program may use at most 192 MiB of HBM per device.

v0:
```python
import math

import jax
import jax.numpy as jnp
from jax import lax
from jax.sharding import PartitionSpec as P

C = 32
M = 16
RD = 128
CD = 512
P_DEV = 1024
MODES = 512


full_turn = 6.283185307179586
exact_mode = lax.Precision.HIGHEST


def row_angles(start_at, extent, period):
    frequency = jnp.arange(2 * M, dtype=jnp.int32)
    frequency = jnp.where(frequency < M, frequency, frequency - 2 * M)
    places = start_at + jnp.arange(extent, dtype=jnp.int32)
    phases = frequency[:, None] * places[None, :] % period
    angles = phases.astype(jnp.float32) * (full_turn / period)
    return (jnp.cos(angles), jnp.sin(angles))


def col_angles(start_at, extent, period):
    frequency = jnp.arange(M, dtype=jnp.int32)
    places = start_at + jnp.arange(extent, dtype=jnp.int32)
    phases = places[:, None] * frequency[None, :] % period
    angles = phases.astype(jnp.float32) * (full_turn / period)
    return (jnp.cos(angles), jnp.sin(angles))


def mode_mask(kept_modes):
    indices = jnp.arange(MODES, dtype=jnp.int32)
    row_mode = indices // M
    col_mode = indices % M
    row_rank = jnp.where(row_mode < M, row_mode, 2 * M - 1 - row_mode)
    allowed = (row_rank[None, :] < kept_modes[:, None]) & (col_mode[None, :] < kept_modes[:, None])
    return allowed.astype(jnp.float32)


def widen(values, full_size, along):
    shape_full = list(values.shape)
    block_size = values.shape[along]
    shape_full[along] = full_size
    holder = jnp.zeros(tuple(shape_full), jnp.float32)
    return lax.dynamic_update_slice_in_dim(holder, values, lax.axis_index("ch") * block_size, along)


def local_modes(own_field, scale_by):
    channel_count, row_count, col_count = own_field.shape
    row_devices = lax.axis_size("row")
    height = row_count * row_devices
    breadth = col_count * lax.axis_size("col")
    row_place = lax.axis_index("row")
    cos_rows, sin_rows = row_angles(row_place * row_count, row_count, height)
    real_rows = jnp.einsum("ar,crs->cas", cos_rows, own_field, precision=exact_mode)
    imag_rows = -jnp.einsum("ar,crs->cas", sin_rows, own_field, precision=exact_mode)
    col_first = lax.axis_index("col") * col_count
    cos_cols, sin_cols = col_angles(col_first, col_count, breadth)
    mode_re = jnp.einsum("cas,sb->cab", real_rows, cos_cols, precision=exact_mode) + jnp.einsum(
        "cas,sb->cab", imag_rows, sin_cols, precision=exact_mode
    )
    mode_im = jnp.einsum("cas,sb->cab", imag_rows, cos_cols, precision=exact_mode) - jnp.einsum(
        "cas,sb->cab", real_rows, sin_cols, precision=exact_mode
    )
    return (
        mode_re.reshape(channel_count, MODES) * scale_by,
        mode_im.reshape(channel_count, MODES) * scale_by,
    )


def tile_field(mode_re, mode_im, scale_by):
    channel_count = mode_re.shape[0]
    grid_re = mode_re.reshape(channel_count, 2 * M, M)
    grid_im = mode_im.reshape(channel_count, 2 * M, M)
    height = RD * lax.axis_size("row")
    breadth = CD * lax.axis_size("col")
    cos_cols, sin_cols = col_angles(lax.axis_index("col") * CD, CD, breadth)
    half_re = jnp.einsum("cab,sb->cas", grid_re, cos_cols, precision=exact_mode) - jnp.einsum(
        "cab,sb->cas", grid_im, sin_cols, precision=exact_mode
    )
    half_im = jnp.einsum("cab,sb->cas", grid_re, sin_cols, precision=exact_mode) + jnp.einsum(
        "cab,sb->cas", grid_im, cos_cols, precision=exact_mode
    )
    cos_rows, sin_rows = row_angles(lax.axis_index("row") * RD, RD, height)
    result = jnp.einsum("ar,cas->crs", cos_rows, half_re, precision=exact_mode) - jnp.einsum(
        "ar,cas->crs", sin_rows, half_im, precision=exact_mode
    )
    return result * scale_by


def per_device(
    field, spec_weight, point_weight, bias, kept_modes, residual, trace_dest, trace_cell
):
    channel_count = C // lax.axis_size("ch")
    own_first = lax.axis_index("ch") * channel_count
    row_devices = lax.axis_size("row")
    col_devices = lax.axis_size("col")
    tiles_all = row_devices * col_devices
    points_all = P_DEV * tiles_all
    capacity = max(2, 2 * P_DEV // tiles_all)
    forward_scale = 1.0 / math.sqrt(RD * row_devices * CD * col_devices)
    mix_scale = 1.0 / math.sqrt(MODES)
    own_field = lax.dynamic_slice_in_dim(field, own_first, channel_count, 0)
    part_re, part_im = local_modes(own_field, forward_scale)
    spec_re, spec_im = lax.psum((widen(part_re, C, 0), widen(part_im, C, 0)), ("row", "col", "ch"))
    allowed = mode_mask(kept_modes)
    weight_re = spec_weight[0] * allowed[None, :, :]
    weight_im = spec_weight[1] * allowed[None, :, :]
    out_wre = lax.dynamic_slice_in_dim(weight_re, own_first, channel_count, 1)
    out_wim = lax.dynamic_slice_in_dim(weight_im, own_first, channel_count, 1)
    mixed_re = jnp.sum(out_wre * spec_re[:, None, :] - out_wim * spec_im[:, None, :], axis=0)
    mixed_im = jnp.sum(out_wre * spec_im[:, None, :] + out_wim * spec_re[:, None, :], axis=0)
    out_point = lax.dynamic_slice_in_dim(point_weight, own_first, channel_count, 1)
    pre_act = (
        tile_field(mixed_re, mixed_im, mix_scale)
        + jnp.einsum("co,crs->ors", out_point, field, precision=exact_mode)
        + bias[:, None, None]
    )
    targets = trace_dest[:, 0]
    one_hot = (targets[:, None] == jnp.arange(tiles_all, dtype=jnp.int32)[None, :]).astype(
        jnp.int32
    )
    earlier = jnp.cumsum(one_hot, axis=0) - one_hot
    slot_rank = jnp.sum(earlier * one_hot, axis=1)
    position = targets * capacity + slot_rank
    send_values = (
        jnp.zeros((channel_count, tiles_all * capacity), jnp.float32).at[:, position].set(residual)
    )
    send_cells = jnp.zeros((tiles_all * capacity,), jnp.int32).at[position].set(trace_cell)
    got_values, got_cells = (
        lax.all_to_all(
            send_values.reshape(channel_count, tiles_all, capacity),
            ("row", "col"),
            split_axis=1,
            concat_axis=1,
            tiled=True,
        ),
        lax.all_to_all(
            send_cells.reshape(1, tiles_all, capacity),
            ("row", "col"),
            split_axis=1,
            concat_axis=1,
            tiled=True,
        ),
    )
    cotangent = (
        jnp.zeros((channel_count, RD * CD), jnp.float32)
        .at[:, got_cells.reshape(-1)]
        .add(got_values.reshape(channel_count, -1))
    )
    cotangent = cotangent.reshape(channel_count, RD, CD)
    out_slope = jax.vjp(jax.nn.gelu, pre_act)[1](cotangent)[0]
    grad_re, grad_im = local_modes(out_slope, mix_scale)
    point_part = jnp.einsum("crs,ors->co", field, out_slope, precision=exact_mode)
    bias_part = jnp.sum(out_slope, axis=(1, 2))
    modes_re, modes_im, point_sum, bias_sum = lax.psum(
        (
            widen(grad_re, C, 0),
            widen(grad_im, C, 0),
            widen(point_part, C, 1),
            widen(bias_part, C, 0),
        ),
        ("row", "col", "ch"),
    )
    own_allowed = lax.dynamic_slice_in_dim(allowed, own_first, channel_count, 0)
    own_gre = lax.dynamic_slice_in_dim(modes_re, own_first, channel_count, 0)
    own_gim = lax.dynamic_slice_in_dim(modes_im, own_first, channel_count, 0)
    grad_scale = math.sqrt(MODES / points_all)
    spec_grad_re = (
        own_allowed[None]
        * (own_gre[None] * spec_re[:, None] + own_gim[None] * spec_im[:, None])
        * grad_scale
    )
    spec_grad_im = (
        own_allowed[None]
        * (own_gim[None] * spec_re[:, None] - own_gre[None] * spec_im[:, None])
        * grad_scale
    )
    grad_spec = jnp.stack((spec_grad_re, spec_grad_im), axis=0)
    in_wre = lax.dynamic_slice_in_dim(weight_re, own_first, channel_count, 0)
    in_wim = lax.dynamic_slice_in_dim(weight_im, own_first, channel_count, 0)
    adjoint_re = jnp.sum(in_wre * modes_re[None] + in_wim * modes_im[None], axis=1)
    adjoint_im = jnp.sum(in_wre * modes_im[None] - in_wim * modes_re[None], axis=1)
    spectral_back = tile_field(adjoint_re, adjoint_im, forward_scale)
    own_point = lax.dynamic_slice_in_dim(point_weight, own_first, channel_count, 1)
    partial_back = jnp.einsum("co,ors->crs", own_point, out_slope, precision=exact_mode)
    point_back = lax.psum_scatter(partial_back, "ch", scatter_dimension=0, tiled=True)
    grad_field = point_back + spectral_back
    norm_points = 1.0 / math.sqrt(points_all)
    grad_point = lax.dynamic_slice_in_dim(point_sum, own_first, channel_count, 1) * norm_points
    grad_bias = lax.dynamic_slice_in_dim(bias_sum, own_first, channel_count, 0) * norm_points
    return (grad_field, grad_spec, grad_point, grad_bias)


def solution(mesh):
    return jax.shard_map(
        per_device,
        mesh=mesh,
        in_specs=(
            P(None, "row", "col"),
            P(),
            P(),
            P("ch"),
            P(),
            P("ch", ("row", "col")),
            P(("row", "col"), None),
            P(("row", "col")),
        ),
        out_specs=(P("ch", "row", "col"), P(None, None, "ch", None), P(None, "ch"), P("ch")),
        check_vma=False,
    )
```

profile of v0, /device:TPU:0, one launch (start us, length us, event | category | flops | bytes accessed | tf_op | source)
XLA Modules:
  0.0 457.2 jit_solution(12711133566505198467)
XLA Ops:
  7.2 0.7 fusion.42
  7.9 4.5 reduce-window.6
  12.8 0.7 fusion.41
  13.5 0.7 compare_select_fusion.1
  14.2 5.0 %scatter_custom_fusion = s32[2048]{0:T(1024)} fusion(s32[1024]{0:T(1024)S(1)} %bitcast.156, s32[1024]{0:T(1024)} %param.15, s32[]{:T(128)} %constant.114.clone.1), kind=kCustom, calls=%fused_computation.137 | custom fusion | bytes 8704 | tf_op jit(solution)/shard_map/scatter | solution.py:135
  19.3 8.3 %all-to-all-start = ((s32[1,16,128]{2,0,1:T(1,128)}), s32[1,16,128]{2,0,1:T(1,128)S(1)}, u32[]{:S(2)}, u32[]{:S(2)}) async-start(s32[1,16,128]{2,0,1:T(1,128)} %bitcast.7), calls=%async_computation | async-start | bytes 16384 | tf_op jit(solution)/shard_map/all_to_all | solution.py:144
  27.7 4.4 fusion.23
  32.1 4.4 fusion.17
  36.5 2.2 fusion.66
  38.7 2.2 fusion.68
  40.9 2.2 fusion.28
  43.3 0.2 mul.415
  43.5 2.2 fusion.27
  45.9 0.2 mul.410
  46.1 0.6 copy-done.6
  46.8 14.1 %fusion.4 = f32[16,128,512]{2,0,1:T(8,128)} fusion(f32[32,128,512]{2,1,0:T(8,128)} %param.8, f32[32,32]{1,0:T(8,128)S(1)} %copy-done, s32[]{:T(128)S(6)} %select_n.97), kind=kOutput, calls=%fused_computation.7 | convolution fusion | flops 402653184 | bytes 12587012 | tf_op jit(solution)/shard_map/co,crs->ors/dot_general | solution.py:122
  61.0 2.1 bitcast_multiply_fusion.1
  63.1 1.0 copy.80
  64.1 3.7 scatter_custom_fusion.1
  67.8 0.9 copy.81
  68.8 5.3 %copy.92 = f32[16,128,512]{1,2,0:T(8,128)} copy(f32[16,128,512]{2,0,1:T(8,128)} %fusion.4) | data formatting | bytes 8388608 | tf_op jit(solution)/shard_map/co,crs->ors/dot_general | solution.py:122
  74.1 7.0 %all-to-all-start.1 = ((f32[16,16,128]{2,0,1:T(8,128)}), f32[16,16,128]{2,0,1:T(8,128)}, u32[]{:S(2)}, u32[]{:S(2)}) async-start(f32[16,16,128]{2,0,1:T(8,128)} %copy.81), calls=%async_computation.1 | async-start | bytes 262144 | tf_op jit(solution)/shard_map/all_to_all | solution.py:137
  81.1 90.1 %all-reduce.8.cloned.1.call-done = (f32[32,512]{1,0:T(8,128)}, f32[32,512]{1,0:T(8,128)}) async-done(((f32[32,512]{1,0:T(8,128)}, f32[32,512]{1,0:T(8,128)}), (f32[32,512]{1,0:T(8,128)}, f32[32,512]{1,0:T(8,128)})) %all-reduce.8.cloned.1.call-update) | async-done | bytes 131088 | tf_op jit(solution)/shard_map/psum | solution.py:111
  171.2 1.6 add_reduce_fusion.1
  172.9 2.1 fusion.64
  175.0 1.1 fusion.51
  176.2 2.3 convolution_subtract_fusion.1
  178.5 8.7 %fusion.87 = f32[16,512,128]{2,1,0:T(8,128)} fusion(f32[16,32,512]{2,1,0:T(8,128)S(1)} %convolution_subtract_fusion.1, s32[128]{0:T(128)S(1)} %iota_add_fusion.1, s32[32]{0:T(128)S(1)} %compare_select_fusion.3), kind=kOutput, calls=%fused_computation.119 | convolution fusion | flops 402710528 | bytes 5243520 | tf_op jit(solution)/shard_map/ar,cas->crs/dot_general | solution.py:91
  187.2 2.1 convolution_add_fusion.1
  189.3 0.9 bitcast_bitcast_fusion
  190.2 0.3 copy.83
  190.5 26.5 %scatter_custom_fusion.2 = f32[16,65536]{0,1:T(8,128)} fusion(s32[2048]{0:T(1024)S(1)} %bitcast.155, f32[2048,16]{1,0:T(8,128)S(1)} %copy.83, f32[]{:T(128)} %constant.118.clone.1), kind=kCustom, calls=%fused_computation.3 | custom fusion | flops 32768 | bytes 4194308 | tf_op jit(solution)/shard_map/scatter-add | solution.py:155
  217.0 19.4 %copy.93 = f32[16,128,512]{1,2,0:T(8,128)} copy(f32[16,128,512]{0,2,1:T(8,128)} %bitcast.147) | data formatting | bytes 8388608 | tf_op jit(solution)/shard_map/reshape | solution.py:157
  236.5 14.2 %fusion.227 = (f32[16]{0:T(128)S(1)}, f32[16,128,512]{1,2,0:T(8,128)}) fusion(f32[16,128,512]{1,2,0:T(8,128)} %copy.93, f32[16]{0:T(128)S(1)} %copy-done.14, f32[16,128,512]{1,2,0:T(8,128)} %copy.92, f32[16,512,128]{2,1,0:T(8,128)} %fusion.87, f32[16,32,512]{2,1,0:T(8,128)S(1)} %copy-done.3, s32[128]{0:T(128)S(1)} %iota_add_fusion.1, ...), kind=kOutput, calls=%fused_computation.252 | convolution fusion | flops 427876352 | bytes 17826560 | tf_op jit(solution)/shard_map/ar,cas->crs/dot_general | solution.py:91
  250.7 5.5 %copy.95 = f32[16,128,512]{2,0,1:T(8,128)} copy(f32[16,128,512]{1,2,0:T(8,128)} %get-tuple-element.35) | data formatting | bytes 8388608 | tf_op jit(solution)/shard_map/transpose(jvp())/add_any | solution.py:158
  256.2 6.8 %fusion.26 = f32[16,32,512]{2,1,0:T(8,128)S(1)} fusion(f32[16,128,512]{1,2,0:T(8,128)} %get-tuple-element.35, s32[128]{0:T(128)S(1)} %iota_add_fusion.1, s32[32]{0:T(128)S(1)} %compare_select_fusion.3), kind=kOutput, calls=%fused_computation.31 | convolution fusion | flops 402972672 | bytes 5243520 | tf_op jit(solution)/shard_map/ar,crs->cas/dot_general | solution.py:62
  263.1 4.6 convolution_bitcast_fusion
  267.6 2.2 fusion.59
  269.8 2.9 fusion.61
  272.7 2.9 fusion.30
  275.6 1.0 copy.99
  276.8 3.1 fusion.29
  280.1 0.2 mul.438
  280.3 0.6 copy-done.8
  281.0 11.0 %fusion.77 = f32[32,128,512]{2,0,1:T(8,128)} fusion(f32[16,128,512]{2,0,1:T(8,128)} %copy.95, f32[32,32]{1,0:T(8,128)S(1)} %copy-done, s32[]{:T(128)S(6)} %select_n.97), kind=kOutput, calls=%fused_computation.109 | convolution fusion | flops 402653184 | bytes 12587012 | tf_op jit(solution)/shard_map/co,ors->crs/dot_general | solution.py:192
  292.1 0.2 dynamic_update_slice.23
  292.3 14.4 %fusion.34 = f32[32,32]{0,1:T(8,128)S(1)} fusion(f32[32,32]{0,1:T(8,128)S(1)} %broadcast_in_dim.10, s32[]{:T(128)S(6)} %select_n.97, f32[16,128,512]{2,0,1:T(8,128)} %copy.95, f32[32,128,512]{2,1,0:T(8,128)} %param.8), kind=kOutput, calls=%fused_computation.46 | convolution fusion | flops 402653184 | bytes 12591108 | tf_op jit(solution)/shard_map/crs,ors->co/dot_general | solution.py:160
  306.8 39.5 %all-reduce = (f32[32,32]{0,1:T(8,128)S(1)}, f32[32]{0:T(128)S(1)}) all-reduce(f32[32,32]{0,1:T(8,128)S(1)} %fusion.34, f32[32]{0:T(128)S(1)} %dynamic_update_slice.23), channel_id=1, replica_groups=mesh['row'=4,'col'=4,'ch'=2] {'row','col','ch'}, use_global_device_ids=true, to_apply=%region_15.16 | all-reduce | flops 1056 | bytes 8448 | tf_op jit(solution)/shard_map/psum | solution.py:162
  346.3 0.6 dynamic-slice_multiply_fusion.1
  346.9 0.6 dynamic-slice_multiply_fusion
  347.5 55.7 %all-reduce.6.cloned.1.call-done = (f32[32,512]{1,0:T(8,128)}, f32[32,512]{1,0:T(8,128)}) async-done(((f32[32,512]{1,0:T(8,128)}, f32[32,512]{1,0:T(8,128)}), (f32[32,512]{1,0:T(8,128)}, f32[32,512]{1,0:T(8,128)})) %all-reduce.6.cloned.1.call-update) | async-done | bytes 131088 | tf_op jit(solution)/shard_map/psum | solution.py:162
  403.1 1.7 subtract_reduce_fusion
  405.0 1.1 fusion.57
  406.1 1.1 convolution_subtract_fusion
  407.2 8.3 %fusion.84 = f32[16,512,128]{2,1,0:T(8,128)} fusion(f32[16,32,512]{2,1,0:T(8,128)S(1)} %convolution_subtract_fusion, s32[128]{0:T(128)S(1)} %iota_add_fusion.1, s32[32]{0:T(128)S(1)} %compare_select_fusion.3), kind=kOutput, calls=%fused_computation.116 | convolution fusion | flops 402710528 | bytes 5243520 | tf_op jit(solution)/shard_map/ar,cas->crs/dot_general | solution.py:91
  415.5 6.0 %copy.104 = f32[16,512,128]{1,0,2:T(8,128)} copy(f32[16,512,128]{2,1,0:T(8,128)} %fusion.84) | data formatting | bytes 8388608 | tf_op jit(solution)/shard_map/ar,cas->crs/dot_general | solution.py:91
  421.6 1.1 fusion.46
  422.6 1.1 convolution_add_fusion
  423.8 8.5 %fusion.79 = f32[16,512,128]{2,1,0:T(8,128)} fusion(f32[16,32,512]{2,1,0:T(8,128)S(1)} %convolution_add_fusion, s32[128]{0:T(128)S(1)} %iota_add_fusion.1, s32[32]{0:T(128)S(1)} %compare_select_fusion.3), kind=kOutput, calls=%fused_computation.111 | convolution fusion | flops 402710528 | bytes 5243520 | tf_op jit(solution)/shard_map/ar,cas->crs/dot_general | solution.py:91
  432.3 5.5 %copy.105 = f32[16,512,128]{1,0,2:T(8,128)} copy(f32[16,512,128]{2,1,0:T(8,128)} %fusion.79) | data formatting | bytes 8388608 | tf_op jit(solution)/shard_map/ar,cas->crs/dot_general | solution.py:91
  437.9 0.3 multiply_multiply_fusion.3
  438.2 1.6 pad_maximum_fusion
  439.8 6.2 %bitcast_add_fusion = f32[16,128,512]{2,0,1:T(8,128)S(1)} fusion(f32[16,128,512]{2,0,1:T(8,128)} %reduce-scatter.2.cloned.1.call-done, f32[16,512,128]{1,0,2:T(8,128)} %copy.104, f32[16,512,128]{1,0,2:T(8,128)} %copy.105), kind=kLoop, calls=%fused_computation.17 | loop fusion | flops 3145728 | bytes 16777216 | tf_op jit(solution)/shard_map/add | solution.py:194
  446.0 4.4 copy.108
  (70 shorter events, 2.0 us)
Async XLA Ops:
  7.2 39.6 %copy-start = (f32[32,32]{1,0:T(8,128)S(1)}, f32[32,32]{1,0:T(8,128)}, u32[]{:S(2)}) copy-start(f32[32,32]{1,0:T(8,128)} %param.10) | copy-start | bytes 12292
  19.3 54.8 %all-to-all-start = ((s32[1,16,128]{2,0,1:T(1,128)}), s32[1,16,128]{2,0,1:T(1,128)S(1)}, u32[]{:S(2)}, u32[]{:S(2)}) async-start(s32[1,16,128]{2,0,1:T(1,128)} %bitcast.7), calls=%async_computation | async-start | bytes 16384 | tf_op jit(solution)/shard_map/all_to_all | solution.py:144
  27.6 143.7 %all-reduce.8.cloned.1.call-start = ((), (), s32[]{:S(2)}) async-start(), calls=%async_computation.5 | async-start | bytes 262144 | tf_op jit(solution)/shard_map/psum | solution.py:111
  46.1 0.6 copy-start.6
  46.1 0.6 copy-start.7
  46.8 14.2 %copy-start.13 = (s32[32]{0:T(128)S(1)}, s32[32]{0:T(128)}, u32[]{:S(2)}) copy-start(s32[32]{0:T(128)} %param.12) | copy-start | bytes 388
  46.8 14.2 %copy-start.2 = (f32[2,32,32,512]{3,2,1,0:T(8,128)S(1)}, f32[2,32,32,512]{3,2,1,0:T(8,128)}, u32[]{:S(2)}) copy-start(f32[2,32,32,512]{3,2,1,0:T(8,128)} %param.9) | copy-start | bytes 12582916
  61.0 2.1 copy-start.12
  74.1 115.2 %all-to-all-start.1 = ((f32[16,16,128]{2,0,1:T(8,128)}), f32[16,16,128]{2,0,1:T(8,128)}, u32[]{:S(2)}, u32[]{:S(2)}) async-start(f32[16,16,128]{2,0,1:T(8,128)} %copy.81), calls=%async_computation.1 | async-start | bytes 262144 | tf_op jit(solution)/shard_map/all_to_all | solution.py:137
  81.1 322.1 %all-reduce.6.cloned.1.call-start = ((), (), s32[]{:S(2)}) async-start(), calls=%async_computation.4 | async-start | bytes 262144 | tf_op jit(solution)/shard_map/psum | solution.py:162
  217.0 19.5 %copy-start.3 = (f32[16,32,512]{2,1,0:T(8,128)S(1)}, f32[16,32,512]{2,1,0:T(8,128)}, u32[]{:S(2)}) copy-start(f32[16,32,512]{2,1,0:T(8,128)} %convolution_add_fusion.1) | copy-start | bytes 3145732
  217.0 19.5 %copy-start.14 = (f32[16]{0:T(128)S(1)}, f32[16]{0:T(128)}, u32[]{:S(2)}) copy-start(f32[16]{0:T(128)} %param.11) | copy-start | bytes 196
  256.2 6.8 %copy-start.1 = (f32[16,128,512]{1,2,0:T(8,128)S(1)}, f32[16,128,512]{1,2,0:T(8,128)}, u32[]{:S(2)}) copy-start(f32[16,128,512]{1,2,0:T(8,128)} %get-tuple-element.35) | copy-start | bytes 12582916
  280.3 0.6 copy-start.8
  280.3 0.6 copy-start.9
  280.9 158.9 %reduce-scatter.2.cloned.1.call-start = ((), (), s32[]{:S(2)}) async-start(), calls=%async_computation.3 | async-start | bytes 12582912 | tf_op jit(solution)/shard_map/reduce_scatter | solution.py:193
  432.3 5.6 %copy-start.11 = (f32[32,512]{1,0:T(8,128)S(1)}, f32[32,512]{1,0:T(8,128)}, u32[]{:S(2)}) copy-start(f32[32,512]{1,0:T(8,128)} %get-tuple-element.26) | copy-start | bytes 196612
  432.3 5.6 %copy-start.10 = (f32[32,512]{1,0:T(8,128)S(1)}, f32[32,512]{1,0:T(8,128)}, u32[]{:S(2)}) copy-start(f32[32,512]{1,0:T(8,128)} %get-tuple-element.27) | copy-start | bytes 196612
  432.3 5.6 %copy-start.4 = (f32[32,512]{1,0:T(8,128)S(1)}, f32[32,512]{1,0:T(8,128)}, u32[]{:S(2)}) copy-start(f32[32,512]{1,0:T(8,128)} %get-tuple-element.28) | copy-start | bytes 196612
  432.3 5.6 %copy-start.5 = (f32[32,512]{1,0:T(8,128)S(1)}, f32[32,512]{1,0:T(8,128)}, u32[]{:S(2)}) copy-start(f32[32,512]{1,0:T(8,128)} %get-tuple-element.29) | copy-start | bytes 196612
Sparse Core Ops, SparseCore 0:
  46.9 124.3 all-reduce.7
  281.1 122.0 all-reduce.5
  405.4 15.7 reduce-scatter.1
where the time goes:
time: 465 us; the launch traced here: 457 us
  waiting for transfers between devices  146 us (31%)
  matrix products  131 us (28%)
  local copies, waits for them, and re-layouts  62.7 us (13%)
  other arithmetic  47.9 us (10%)
  blocking collectives  39.5 us (8%)
  starting transfers between devices  15.4 us (3%)
  between operations  14.5 us (3%)
    psum x1, waiting for transfers between devices, per_device(): lax.psum((widen(part_re, C, 0), widen(part_im, C, 0)), ('row', 'col', 'ch'))  90.1 us
    psum x1, waiting for transfers between devices, per_device(): lax.psum((widen(grad_re, C, 0), widen(grad_im, C, 0), widen(point_part, C...  55.7 us
    psum x1, blocking collectives, per_device(): lax.psum((widen(grad_re, C, 0), widen(grad_im, C, 0), widen(point_part, C...  39.5 us
    scatter-add x1, other arithmetic, per_device(): cotangent = jnp.zeros((channel_count, RD * CD), jnp.float32).at[:, got_ce...  26.5 us
    dot_general x2, matrix products, tile_field(): jnp.einsum('ar,cas->crs', sin_rows, half_im, precision=exact_mode)  22.7 us
    reshape x1, local copies, waits for them, and re-layouts, per_device(): cotangent = cotangent.reshape(channel_count, RD, CD)  19.4 us
    dot_general x2, matrix products, tile_field(): jnp.einsum('ar,cas->crs', cos_rows, half_re, precision=exact_mode)  17 us
    dot_general x1, matrix products, per_device(): jnp.einsum('crs,ors->co', field, out_slope, precision=exact_mode)  14.4 us
  transfers between devices with their start and end apart: 5, of which 2 were waited for; matrix products, arithmetic and copies ran while one was open for 28% of the time, Pallas kernels for 0%

commit v1 on v0

v1 whole, which is shorter than its diff:
```python
import functools
import math

import jax
import jax.numpy as jnp
from jax import lax
from jax.experimental import pallas as pl
from jax.experimental.pallas import tpu as pltpu
from jax.sharding import PartitionSpec as P

M = 16
A = 2 * M
MODES = A * M
RB = 8
F32 = jnp.float32
BF16 = jnp.bfloat16
FULL_TURN = 6.283185307179586
NN = (((1,), (0,)), ((), ()))
NT = (((1,), (1,)), ((), ()))
MIB = 1 << 20


def row_table(start_at, extent, period):
    frequency = jnp.arange(A, dtype=jnp.int32)
    frequency = jnp.where(frequency < M, frequency, frequency - A)
    places = start_at + jnp.arange(extent, dtype=jnp.int32)
    phases = frequency[:, None] * places[None, :] % period
    angles = phases.astype(F32) * (FULL_TURN / period)
    return jnp.concatenate((jnp.cos(angles), jnp.sin(angles)), axis=0)


def col_table(start_at, extent, period):
    frequency = jnp.arange(M, dtype=jnp.int32)
    places = start_at + jnp.arange(extent, dtype=jnp.int32)
    phases = frequency[:, None] * places[None, :] % period
    angles = phases.astype(F32) * (FULL_TURN / period)
    return jnp.concatenate((jnp.cos(angles), jnp.sin(angles)), axis=0)


def mode_mask(kept_modes):
    indices = jnp.arange(MODES, dtype=jnp.int32)
    row_mode = indices // M
    col_mode = indices % M
    row_rank = jnp.where(row_mode < M, row_mode, 2 * M - 1 - row_mode)
    allowed = (row_rank[None, :] < kept_modes[:, None]) & (col_mode[None, :] < kept_modes[:, None])
    return allowed.astype(F32)


def split2(x):
    hi = x.astype(BF16)
    return hi, (x - hi.astype(F32)).astype(BF16)


def mm(a, b, dims=NN):
    return lax.dot_general(a, b, dims, preferred_element_type=F32)


def dot3(a, b, dims=NN):
    return mm(a[0], b[0], dims) + (mm(a[0], b[1], dims) + mm(a[1], b[0], dims))


def pack_kernel(tiles, cap, dest_ref, vals_ref, out_ref):
    n = dest_ref.shape[0]
    dest = dest_ref[...]
    wide = max(tiles, 128)
    named = dest == lax.broadcasted_iota(jnp.int32, (n, wide), 1)
    one_hot = named.astype(F32).astype(BF16)
    before = (
        lax.broadcasted_iota(jnp.int32, (n, n), 1) < lax.broadcasted_iota(jnp.int32, (n, n), 0)
    )
    earlier = mm(before.astype(F32).astype(BF16), one_hot)
    rank = jnp.sum(jnp.where(named, earlier, 0.0), axis=1, keepdims=True)
    position = dest * cap + rank.astype(jnp.int32)
    vals = vals_ref[...]
    rows = vals.shape[0]
    hi = vals.astype(BF16)
    left = vals - hi.astype(F32)
    mid = left.astype(BF16)
    low = (left - mid.astype(F32)).astype(BF16)
    parts = jnp.concatenate((hi.astype(F32), mid.astype(F32), low.astype(F32)), axis=0).astype(BF16)
    step = 512
    for first in range(0, tiles * cap, step):
        at = lax.broadcasted_iota(jnp.int32, (n, step), 1) + first
        place = (position == at).astype(F32).astype(BF16)
        got = mm(parts, place)
        out_ref[:, first : first + step] = (
            got[:rows] + got[rows : 2 * rows] + got[2 * rows : 3 * rows]
        )


def pack_points(dest, vals, tiles, cap):
    return pl.pallas_call(
        functools.partial(pack_kernel, tiles, cap),
        out_shape=jax.ShapeDtypeStruct((vals.shape[0], tiles * cap), F32),
        compiler_params=pltpu.CompilerParams(vmem_limit_bytes=40 * MIB),
    )(dest, vals)


def to_modes(rows2, tall, out_ref, at, scale):
    grid = dot3(rows2, split2(tall))
    out_ref[at, 0] = (grid[:A, :M] - grid[A:, M:]) * scale
    out_ref[at, 1] = (grid[A:, :M] + grid[:A, M:]) * (-scale)


def field_modes_kernel(scale, own_ref, field_ref, cols_ref, rows_ref, out_ref):
    count, height, width = field_ref.shape
    cols2 = split2(cols_ref[...])
    rows2 = split2(rows_ref[...])
    tall = dot3(split2(field_ref[...].reshape(count * height, width)), cols2)
    for c in range(count):
        to_modes(rows2, tall[c * height : (c + 1) * height], out_ref, c, scale)


def field_modes(field, own, own_count, cols, rows, scale):
    _, height, width = field.shape
    count = 4
    steps = own_count // count
    return pl.pallas_call(
        functools.partial(field_modes_kernel, scale),
        grid_spec=pltpu.PrefetchScalarGridSpec(
            num_scalar_prefetch=1,
            grid=(steps,),
            in_specs=[
                pl.BlockSpec((count, height, width), lambda i, own: (own[0] * steps + i, 0, 0)),
                pl.BlockSpec(cols.shape, lambda i, own: (0, 0)),
                pl.BlockSpec(rows.shape, lambda i, own: (0, 0)),
            ],
            out_specs=pl.BlockSpec((count, 2, A, M), lambda i, own: (i, 0, 0, 0)),
        ),
        out_shape=jax.ShapeDtypeStruct((own_count, 2, A, M), F32),
        compiler_params=pltpu.CompilerParams(vmem_limit_bytes=40 * MIB),
    )(own, field, cols, rows)


def slope_kernel(
    scale, field_ref, grid_ref, tall_rows_ref, wide_cols_ref, tall_cols_ref, rows_ref, kron_ref,
    bias_ref, vals_ref, rowid_ref, colid_ref, group_ref,
    slope_ref, modes_ref, point_ref,
    half_ref, hot_ref, vhi_ref, vlo_ref, tall_ref, acc_ref,
):
    step = pl.program_id(0)
    channels, _, width = slope_ref.shape
    rows = channels * RB
    points = vals_ref.shape[1]
    inputs = field_ref.shape[0]

    @pl.when(step == 0)
    def _():
        tall_rows = split2(tall_rows_ref[...])
        for o in range(channels):
            half_ref[o] = dot3(tall_rows, split2(grid_ref[o]))
        vals = vals_ref[...]
        hi = vals.astype(BF16).astype(F32)
        low = vals - hi
        vhi_ref[...] = jnp.broadcast_to(hi[:, None, :], (channels, RB, points)).reshape(rows, points)
        vlo_ref[...] = jnp.broadcast_to(low[:, None, :], (channels, RB, points)).reshape(rows, points)
        part = 256
        for first in range(0, points, part):
            ids = colid_ref[first : first + part, :]
            hot = ids == lax.broadcasted_iota(jnp.int32, (part, width), 1)
            hot_ref[first : first + part, :] = hot.astype(F32).astype(BF16)
        acc_ref[...] = jnp.zeros_like(acc_ref)

    block2 = split2(field_ref[...].reshape(inputs * RB, width))
    half = half_ref[:, pl.ds(pl.multiple_of(step * RB, RB), RB), :].reshape(rows, 2 * M)
    pre = (
        dot3(split2(half), split2(wide_cols_ref[...]))
        + dot3(split2(kron_ref[...]), block2)
        + bias_ref[...]
    )
    here = rowid_ref[...] == step * RB + lax.broadcasted_iota(jnp.int32, (RB, points), 0)
    here = jnp.broadcast_to(here.astype(F32)[None], (channels, RB, points)).reshape(rows, points)
    cot = mm((vhi_ref[...] * here).astype(BF16), hot_ref[...]) + mm(
        (vlo_ref[...] * here).astype(BF16), hot_ref[...]
    )
    k = math.sqrt(2.0 / math.pi)
    square = pre * pre
    t = jnp.tanh(k * pre * (1.0 + 0.044715 * square))
    rate = 0.5 * (1.0 + t) + 0.5 * k * pre * (1.0 - t * t) * (1.0 + 3 * 0.044715 * square)
    slope = cot * rate
    slope_ref[...] = slope.reshape(channels, RB, width)
    slope2 = split2(slope)
    tall = dot3(slope2, split2(tall_cols_ref[...]))
    tall_ref[:, pl.ds(pl.multiple_of(step * RB, RB), RB), :] = tall.reshape(channels, RB, 2 * M)
    acc_ref[...] += dot3(block2, slope2, NT)

    @pl.when(step == pl.num_programs(0) - 1)
    def _():
        rows2 = split2(rows_ref[...])
        for o in range(channels):
            to_modes(rows2, tall_ref[o], modes_ref, o, scale)
        total = acc_ref[...]
        same = lax.broadcasted_iota(jnp.int32, total.shape, 0) % RB == (
            lax.broadcasted_iota(jnp.int32, total.shape, 1) % RB
        )
        kept = jnp.sum(jnp.where(same, total, 0.0).reshape(inputs, RB, rows), axis=1)
        point_ref[...] = lax.dot_general(
            kept, group_ref[...], NN, precision=lax.Precision.HIGHEST, preferred_element_type=F32
        )


def whole(shape):
    return pl.BlockSpec(shape, lambda i: (0,) * len(shape))


def slope_pass(field, grid, wide_cols, cols_t, rows, rows_t, kron, bias, vals, rowid, colid, scale):
    inputs, height, width = field.shape
    channels = grid.shape[0]
    points = vals.shape[1]
    lanes = channels * RB
    group = (
        jnp.arange(lanes, dtype=jnp.int32)[:, None] // RB
        == jnp.arange(channels, dtype=jnp.int32)[None, :]
    ).astype(F32)
    args = (field, grid, rows_t, wide_cols, cols_t, rows, kron, bias, vals, rowid, colid, group)
    return pl.pallas_call(
        functools.partial(slope_kernel, scale),
        grid=(height // RB,),
        in_specs=[pl.BlockSpec((inputs, RB, width), lambda i: (0, i, 0))]
        + [whole(arg.shape) for arg in args[1:]],
        out_specs=[
            pl.BlockSpec((channels, RB, width), lambda i: (0, i, 0)),
            whole((channels, 2, A, M)),
            whole((inputs, channels)),
        ],
        out_shape=[
            jax.ShapeDtypeStruct((channels, height, width), F32),
            jax.ShapeDtypeStruct((channels, 2, A, M), F32),
            jax.ShapeDtypeStruct((inputs, channels), F32),
        ],
        scratch_shapes=[
            pltpu.VMEM((channels, height, 2 * M), F32),
            pltpu.VMEM((points, width), BF16),
            pltpu.VMEM((lanes, points), F32),
            pltpu.VMEM((lanes, points), F32),
            pltpu.VMEM((channels, height, 2 * M), F32),
            pltpu.VMEM((inputs * RB, lanes), F32),
        ],
        compiler_params=pltpu.CompilerParams(vmem_limit_bytes=52 * MIB),
    )(*args)


def back_kernel(
    own_ref, other_ref, grid_ref, tall_rows_ref, wide_cols_ref, kron_own_ref, kron_other_ref,
    out_ref, half_ref,
):
    step = pl.program_id(0)
    channels, block, width = out_ref.shape
    rows = channels * RB

    @pl.when(step == 0)
    def _():
        tall_rows = split2(tall_rows_ref[...])
        for c in range(channels):
            half_ref[c] = dot3(tall_rows, split2(grid_ref[c]))

    half = half_ref[:, pl.ds(pl.multiple_of(step * RB, RB), RB), :].reshape(rows, 2 * M)
    result = (
        dot3(split2(half), split2(wide_cols_ref[...]))
        + dot3(split2(kron_own_ref[...]), split2(own_ref[...].reshape(rows, width)))
        + dot3(split2(kron_other_ref[...]), split2(other_ref[...].reshape(rows, width)))
    )
    out_ref[...] = result.reshape(channels, RB, width)


def back_pass(own, other, grid, rows_t, wide_cols, kron_own, kron_other):
    channels, height, width = own.shape
    args = (own, other, grid, rows_t, wide_cols, kron_own, kron_other)
    block = pl.BlockSpec((channels, RB, width), lambda i: (0, i, 0))
    return pl.pallas_call(
        back_kernel,
        grid=(height // RB,),
        in_specs=[block, block] + [whole(arg.shape) for arg in args[2:]],
        out_specs=block,
        out_shape=jax.ShapeDtypeStruct((channels, height, width), F32),
        scratch_shapes=[pltpu.VMEM((channels, height, 2 * M), F32)],
        compiler_params=pltpu.CompilerParams(vmem_limit_bytes=40 * MIB),
    )(*args)


def sum_kernel(n_row, n_col, x_ref, out_ref, landed, total, gathered, send1, recv1, send2, recv2):
    n = n_row * n_col
    row = lax.axis_index("row")
    col = lax.axis_index("col")
    ch = lax.axis_index("ch")
    me = row * n_col + col

    def device(offset, flip):
        at = lax.rem(me + offset, n)
        return (at // n_col, lax.rem(at, n_col), lax.rem(ch + flip, 2))

    barrier = pltpu.get_barrier_semaphore()

    def greet(i, carry):
        pl.semaphore_signal(
            barrier, inc=1, device_id=device(i // 2, lax.rem(i, 2)),
            device_id_type=pl.DeviceIdType.MESH,
        )
        return carry

    lax.fori_loop(1, 2 * n, greet, 0)
    pl.semaphore_wait(barrier, 2 * n - 1)

    def scatter(k):
        return pltpu.make_async_remote_copy(
            src_ref=x_ref.at[lax.rem(me + k, n)],
            dst_ref=landed.at[k],
            send_sem=send1.at[k],
            recv_sem=recv1.at[k],
            device_id=device(k, 0),
            device_id_type=pl.DeviceIdType.MESH,
        )

    def start1(k, carry):
        scatter(k).start()
        return carry

    lax.fori_loop(1, n, start1, 0)
    total[...] = x_ref[me]

    def take(k, carry):
        scatter(k).wait_recv()
        total[...] += landed[k]
        return carry

    lax.fori_loop(1, n, take, 0)
    gathered[ch * n + me] = total[...]

    def spread(i):
        return pltpu.make_async_remote_copy(
            src_ref=total,
            dst_ref=gathered.at[ch * n + me],
            send_sem=send2.at[i],
            recv_sem=recv2.at[i],
            device_id=device(i // 2, lax.rem(i, 2)),
            device_id_type=pl.DeviceIdType.MESH,
        )

    def start2(i, carry):
        spread(i).start()
        return carry

    lax.fori_loop(1, 2 * n, start2, 0)

    def end1(k, carry):
        scatter(k).wait_send()
        return carry

    lax.fori_loop(1, n, end1, 0)

    def end2(i, carry):
        spread(i).wait()
        return carry

    lax.fori_loop(1, 2 * n, end2, 0)
    out_ref[...] = gathered[...]


def device_sum(x, n_row, n_col, which):
    n = n_row * n_col
    size = x.shape[0]
    tall = -(-size // (n * 128))
    x = jnp.pad(x, (0, n * tall * 128 - size)).reshape(n, tall, 128)
    out = pl.pallas_call(
        functools.partial(sum_kernel, n_row, n_col),
        out_shape=jax.ShapeDtypeStruct((2 * n, tall, 128), F32),
        in_specs=[pl.BlockSpec(memory_space=pltpu.VMEM)],
        out_specs=pl.BlockSpec(memory_space=pltpu.VMEM),
        scratch_shapes=[
            pltpu.VMEM((n, tall, 128), F32),
            pltpu.VMEM((tall, 128), F32),
            pltpu.VMEM((2 * n, tall, 128), F32),
            pltpu.SemaphoreType.DMA((n,)),
            pltpu.SemaphoreType.DMA((n,)),
            pltpu.SemaphoreType.DMA((2 * n,)),
            pltpu.SemaphoreType.DMA((2 * n,)),
        ],
        compiler_params=pltpu.CompilerParams(collective_id=which, has_side_effects=True),
    )(x)
    return out.reshape(2, n * tall * 128)[:, :size]


def mode_grid(re, im):
    count = re.shape[0]
    re = re.reshape(count, A, M)
    im = im.reshape(count, A, M)
    return jnp.concatenate(
        (jnp.concatenate((re, im), axis=2), jnp.concatenate((-im, re), axis=2)), axis=1
    )


def spread_rows(weights):
    eye = jnp.eye(RB, dtype=F32)
    a, b = weights.shape
    return (weights[:, None, :, None] * eye[None, :, None, :]).reshape(a * RB, b * RB)


def per_device(
    field, spec_weight, point_weight, bias, kept_modes, residual, trace_dest, trace_cell
):
    n_row = lax.axis_size("row")
    n_col = lax.axis_size("col")
    ch = lax.axis_index("ch")
    inputs, height, width = field.shape
    own = inputs // lax.axis_size("ch")
    first = ch * own
    points = trace_dest.shape[0]
    tiles = n_row * n_col
    points_all = points * tiles
    cap = max(2, 2 * points // tiles)
    forward_scale = 1.0 / math.sqrt(height * n_row * width * n_col)
    mix_scale = 1.0 / math.sqrt(MODES)

    rows = row_table(lax.axis_index("row") * height, height, height * n_row)
    cols = col_table(lax.axis_index("col") * width, width, width * n_col)
    rows_t = rows.T
    cols_t = cols.T
    wide_cols = jnp.concatenate((cols[:M], -cols[M:]), axis=0)

    vals = jnp.concatenate(
        (residual, (trace_cell + 1).astype(F32)[None, :], jnp.zeros((7, points), F32)), axis=0
    )
    packed = pack_points(trace_dest, vals, tiles, cap)
    packed = packed.reshape(own + 8, tiles, cap).transpose(1, 0, 2)
    got = lax.all_to_all(packed, ("row", "col"), split_axis=0, concat_axis=0, tiled=True)
    got = got.transpose(1, 0, 2).reshape(own + 8, tiles * cap)
    cell = got[own].astype(jnp.int32) - 1
    rowid = jnp.where(cell < 0, -1, cell // width)[None, :]
    colid = jnp.where(cell < 0, -1, cell % width)[:, None]

    part = field_modes(field, ch.reshape(1), own, cols_t, rows, forward_scale)
    spec = device_sum(part.reshape(-1), n_row, n_col, 0).reshape(inputs, 2, MODES)
    spec_re, spec_im = spec[:, 0], spec[:, 1]

    allowed = mode_mask(kept_modes)
    own_allowed = lax.dynamic_slice_in_dim(allowed, first, own, 0)
    out_w = lax.dynamic_slice_in_dim(spec_weight, first, own, 2)
    mixed_re = own_allowed * jnp.sum(
        out_w[0] * spec_re[:, None, :] - out_w[1] * spec_im[:, None, :], axis=0
    )
    mixed_im = own_allowed * jnp.sum(
        out_w[0] * spec_im[:, None, :] + out_w[1] * spec_re[:, None, :], axis=0
    )
    kron = spread_rows(lax.dynamic_slice_in_dim(point_weight, first, own, 1).T)
    slope, grad_part, point_part = slope_pass(
        field, mode_grid(mixed_re * mix_scale, mixed_im * mix_scale), wide_cols, cols_t, rows,
        rows_t, kron, jnp.repeat(bias, RB)[:, None], got[:own], rowid, colid, mix_scale,
    )
    swap = [(0, 1), (1, 0)]
    other_slope = lax.ppermute(slope, "ch", swap)

    summed = device_sum(
        jnp.concatenate((grad_part.reshape(-1), point_part.reshape(-1))), n_row, n_col, 1
    )
    mode_size = own * 2 * MODES
    modes = summed[:, :mode_size].reshape(inputs, 2, MODES)
    modes_re, modes_im = modes[:, 0], modes[:, 1]
    mine = lax.dynamic_slice_in_dim(summed, ch, 1, 0)[0]
    own_modes = mine[:mode_size].reshape(own, 2, MODES)
    own_gre, own_gim = own_modes[:, 0], own_modes[:, 1]
    norm_points = 1.0 / math.sqrt(points_all)
    grad_point = mine[mode_size:].reshape(inputs, own) * norm_points
    grad_bias = own_gre[:, 0] * (norm_points / mix_scale)

    grad_scale = math.sqrt(MODES / points_all)
    keep_re = own_allowed * own_gre * grad_scale
    keep_im = own_allowed * own_gim * grad_scale
    grad_spec = jnp.stack(
        (
            keep_re[None] * spec_re[:, None] + keep_im[None] * spec_im[:, None],
            keep_im[None] * spec_re[:, None] - keep_re[None] * spec_im[:, None],
        ),
        axis=0,
    )
    in_w = lax.dynamic_slice_in_dim(spec_weight, first, own, 1)
    all_re = allowed * modes_re * forward_scale
    all_im = allowed * modes_im * forward_scale
    adjoint_re = jnp.sum(in_w[0] * all_re[None] + in_w[1] * all_im[None], axis=1)
    adjoint_im = jnp.sum(in_w[0] * all_im[None] - in_w[1] * all_re[None], axis=1)
    own_point = lax.dynamic_slice_in_dim(point_weight, first, own, 0)
    kron_own = spread_rows(lax.dynamic_slice_in_dim(own_point, first, own, 1))
    kron_other = spread_rows(lax.dynamic_slice_in_dim(own_point, own - first, own, 1))
    grad_field = back_pass(
        slope, other_slope, mode_grid(adjoint_re, adjoint_im), rows_t, wide_cols, kron_own,
        kron_other,
    )
    return (grad_field, grad_spec, grad_point, grad_bias)


def solution(mesh):
    return jax.shard_map(
        per_device,
        mesh=mesh,
        in_specs=(
            P(None, "row", "col"),
            P(),
            P(),
            P("ch"),
            P(),
            P("ch", ("row", "col")),
            P(("row", "col"), None),
            P(("row", "col")),
        ),
        out_specs=(P("ch", "row", "col"), P(None, None, "ch", None), P(None, "ch"), P("ch")),
        check_vma=False,
    )
```

time: 465 us -> 118 us (0.25); the launches traced: 457 us -> 118 us
  waiting for transfers between devices: 146 us -> 0.01 us
  matrix products: 131 us -> 0 us
  Pallas kernels: 0 us -> 78.8 us
  local copies, waits for them, and re-layouts: 62.7 us -> 17 us
  blocking collectives: 39.5 us -> 0 us
  other arithmetic: 47.9 us -> 12 us
  between operations: 14.5 us -> 1.24 us
  starting transfers between devices: 15.4 us -> 8.43 us
    psum x2 -> x0, waiting for transfers between devices: 146 us -> none  [the longest x1 90.1 us: per_device(): lax.psum((widen(part_re, C, 0), widen(part_im, C, 0)), ('row', 'col', 'ch'))]
    dot_general x27 -> x0, matrix products: 131 us -> none  [the longest x2 22.7 us: tile_field(): jnp.einsum('ar,cas->crs', sin_rows, half_im, precision=exact_mode)]
    pallas_call x0 -> x6, Pallas kernels: none -> 78.8 us  [the longest x2 31.5 us: device_sum(): pl.pallas_call(functools.partial(sum_kernel, n_row, n_col), out_shape=jax...]
    psum x1 -> x0, blocking collectives: 39.5 us -> none  [per_device(): lax.psum((widen(grad_re, C, 0), widen(grad_im, C, 0), widen(point_part, C...]
    scatter-add x1 -> x0, other arithmetic: 26.5 us -> none  [per_device(): cotangent = jnp.zeros((channel_count, RD * CD), jnp.float32).at[:, got_ce...]
    reshape x8 -> x11, local copies, waits for them, and re-layouts: 22.1 us -> 3.46 us  [the longest x2 1.48 us: device_sum(): x = jnp.pad(x, (0, n * tall * 128 - size)).reshape(n, tall, 128)]
    dot_general x3 -> x0, local copies, waits for them, and re-layouts: 16.9 us -> none  [the longest x1 6.03 us: tile_field(): jnp.einsum('ar,cas->crs', cos_rows, half_re, precision=exact_mode)]
    scatter x2 -> x0, local copies, waits for them, and re-layouts: 8.78 us -> none  [the longest x1 5.04 us: per_device(): jnp.zeros((tiles_all * capacity,), jnp.int32).at[position].set(trace_cell)]
  transfers between devices with their start and end apart: 5 -> 2, of which waited for: 2 -> 0; matrix products, arithmetic and copies ran while one was open for 28% -> 15% of each run, Pallas kernels for 0% -> 30%
where the time goes in v1:
time: 118 us
  Pallas kernels  78.8 us (67%)
  local copies, waits for them, and re-layouts  17 us (14%)
  other arithmetic  12 us (10%)
  starting transfers between devices  8.43 us (7%)
  between operations  1.24 us (1%)
    pallas_call x2, Pallas kernels, device_sum(): pl.pallas_call(functools.partial(sum_kernel, n_row, n_col), out_shape=jax...  31.5 us
    pallas_call x1, Pallas kernels, slope_pass(): pl.pallas_call(functools.partial(slope_kernel, scale), grid=(height // RB...  26.3 us
    pallas_call x1, Pallas kernels, back_pass(): pl.pallas_call(back_kernel, grid=(height // RB,), in_specs=[block, block]...  13.9 us
    all_to_all x1, starting transfers between devices, per_device(): lax.all_to_all(packed, ('row', 'col'), split_axis=0, concat_axis=0, tiled...  8.37 us
    unnamed x33, local copies, waits for them, and re-layouts  6.4 us
    pallas_call x1, Pallas kernels, field_modes(): pl.pallas_call(functools.partial(field_modes_kernel, scale), grid_spec=pl...  3.84 us
    pallas_call x1, Pallas kernels, pack_points(): pl.pallas_call(functools.partial(pack_kernel, tiles, cap), out_shape=jax....  3.29 us
  transfers between devices with their start and end apart: 2, of which 0 were waited for; matrix products, arithmetic and copies ran while one was open for 15% of the time, Pallas kernels for 30%

profile of v1, /device:TPU:0, one launch (start us, length us, event | category | flops | bytes accessed | tf_op | source)
XLA Modules:
  0.0 117.5 jit_solution(6953298347166153140)
XLA Ops:
  0.6 0.9 copy.73.dest_ref
  1.5 0.7 add_convert_fusion
  2.2 0.1 pad.15.clone
  2.3 0.9 maximum_maximum_fusion.2.vals_ref
  3.2 3.3 %shard_map.113 = f32[24,2048]{1,0:T(8,128)S(1)} custom-call(s32[1024,1]{1,0:T(8,128)S(1)} %copy.73.dest_ref, f32[24,1024]{1,0:T(8,128)S(1)} %maximum_maximum_fusion.2.vals_ref), custom_call_target="tpu_custom_call" | custom-call | tf_op jit(solution)/shard_map/pallas_call | solution.py:92
  6.5 0.7 bitcast_bitcast_fusion
  7.2 8.4 %all-to-all-start = ((f32[16,24,128]{2,1,0:T(8,128)}), f32[16,24,128]{2,1,0:T(8,128)}, u32[]{:S(2)}, u32[]{:S(2)}) async-start(f32[16,24,128]{2,1,0:T(8,128)} %bitcast_bitcast_fusion), calls=%async_computation | async-start | bytes 393216 | tf_op jit(solution)/shard_map/all_to_all | solution.py:425
  15.7 0.1 fusion.17
  15.7 0.1 copy.69
  15.8 0.2 multiply_cosine_fusion
  16.1 0.1 pad_maximum_fusion.3
  16.2 0.1 fusion.38.tall_rows_ref
  16.3 0.1 fusion.21
  16.5 0.1 copy.70.cols_ref.tall_cols_ref
  16.6 0.1 copy.71.rows_ref
  16.7 3.4 %copy-done = f32[32,128,512]{2,1,0:T(8,128)S(1)} copy-done((f32[32,128,512]{2,1,0:T(8,128)S(1)}, f32[32,128,512]{2,1,0:T(8,128)}, u32[]{:S(2)}) %copy-start) | copy-done | bytes 8388632
  20.1 3.8 %shard_map.111 = f32[16,2,32,16]{3,2,1,0:T(8,128)S(1)} custom-call(s32[1]{0:T(128)} %bitcast.1.own_ref, f32[32,128,512]{2,1,0:T(8,128)S(1)} %copy-done, f32[512,32]{1,0:T(8,128)S(1)} %copy.70.cols_ref.tall_cols_ref, f32[64,128]{1,0:T(8,128)S(1)} %copy.71.rows_ref), custom_call_target="tpu_custom_call" | custom-call | tf_op jit(solution)/shard_map/pallas_call | solution.py:118
  24.0 0.8 reshape.409.x_ref
  24.8 17.3 %shard_map.112 = f32[32,8,128]{2,1,0:T(8,128)} custom-call(f32[16,8,128]{2,1,0:T(8,128)} %reshape.409.x_ref), custom_call_target="tpu_custom_call" | custom-call | tf_op jit(solution)/shard_map/pallas_call | solution.py:364
  42.1 1.0 reshape_reshape.3
  43.0 0.1 fusion.35
  43.2 0.1 dynamic-slice_bitcast_fusion.4
  43.2 0.1 copy.72
  43.4 0.3 broadcast_multiply_fusion
  43.7 0.1 compare_and_fusion
  43.8 1.9 %add_reduce_fusion.1 = (f32[16,512]{1,0:T(8,128)S(1)}, f32[16,512]{1,0:T(8,128)S(1)}) fusion(f32[2,32,32,512]{3,2,1,0:T(8,128)} %param.9, s32[]{:T(128)S(6)} %select_n.124, s32[]{:T(128)S(6)} %add.160, f32[32,512]{1,0:T(8,128)S(1)} %get-tuple-element.57, f32[32,512]{1,0:T(8,128)S(1)} %get-tuple-element.58), kind=kLoop, calls=%fused_computation.15 | loop fusion | flops 2080768 | bytes 2293768 | tf_op jit(solution)/shard_map/reduce_sum | solution.py:441
  45.7 0.5 and_select_fusion.1
  46.2 0.1 reshape.410
  46.4 0.1 reshape.411
  46.5 1.2 %mul.317.kron_ref = f32[128,256]{1,0:T(8,128)S(1)} reshape(f32[16,8,32,8]{3,2,1,0:T(8,128)S(1)} %broadcast_multiply_fusion) | data formatting | bytes 262144 | tf_op jit(solution)/shard_map/mul | solution.py:395
  47.7 0.7 broadcast_in_dim.9
  48.5 0.1 broadcast_in_dim_reshape.4.bias_ref
  48.6 0.2 maximum_maximum_fusion.grid_ref
  48.8 0.1 fusion.6.group_ref
  48.9 1.0 copy.111
  50.0 0.4 copy.76
  50.3 1.4 %compare_select_fusion.colid_ref = s32[2048,1]{1,0:T(8,128)} fusion(s32[2048,1]{1,0:T(8,128)S(1)} %copy.76), kind=kLoop, calls=%fused_computation.5 | loop fusion | flops 24576 | bytes 16384 | tf_op jit(solution)/shard_map/jit(_where)/select_n | solution.py:429
  51.7 26.3 %shard_map.114 = (f32[16,128,512]{2,1,0:T(8,128)}, f32[16,2,32,16]{3,2,1,0:T(8,128)S(1)}, f32[32,16]{1,0:T(8,128)S(1)}) custom-call(f32[32,128,512]{2,1,0:T(8,128)} %field_ref.3, f32[16,64,32]{2,1,0:T(8,128)S(1)} %maximum_maximum_fusion.grid_ref, f32[128,64]{1,0:T(8,128)S(1)} %fusion.38.tall_rows_ref, f32[32,512]{1,0:T(8,128)S(1)} %get-tuple-element.40.wide_cols_ref, ...), custom_call_target="tpu_custom_call" | custom-call | tf_op jit(solution)/shard_map/pallas_call | solution.py:216
  78.0 0.1 collective-permute-start
  78.1 0.1 fusion.37
  78.2 0.2 broadcast_multiply_fusion.1
  78.4 0.5 mul.331.kron_own_ref
  78.9 0.5 mul.334.kron_other_ref
  79.4 0.1 reshape.414
  79.5 0.2 reshape.413
  79.7 0.7 reshape.415.x_ref
  80.4 14.2 %shard_map.115 = f32[32,9,128]{2,1,0:T(8,128)} custom-call(f32[16,9,128]{2,1,0:T(8,128)} %reshape.415.x_ref), custom_call_target="tpu_custom_call" | custom-call | tf_op jit(solution)/shard_map/pallas_call | solution.py:364
  94.6 1.0 reshape.416
  95.7 0.2 reshape.417
  95.8 0.1 fusion.34
  96.0 0.1 fusion.4
  96.1 1.9 %subtract_reduce_fusion = (f32[16,512]{1,0:T(8,128)S(1)}, f32[16,512]{1,0:T(8,128)S(1)}) fusion(f32[2,32,32,512]{3,2,1,0:T(8,128)} %param.9, s32[]{:T(128)S(6)} %select_n.124, s32[]{:T(128)S(6)} %add.160, f32[32,512]{1,0:T(8,128)S(1)} %get-tuple-element.49, f32[32,512]{1,0:T(8,128)S(1)} %get-tuple-element.48), kind=kLoop, calls=%fused_computation.12 | loop fusion | flops 2080768 | bytes 2293768 | tf_op jit(solution)/shard_map/reduce_sum | solution.py:479
  98.0 0.1 reshape.418
  98.1 0.1 reshape.419
  98.3 0.2 dynamic-slice_reduce_fusion
  98.5 0.1 fusion.31
  98.6 0.1 mul.349
  98.7 0.7 copy.85
  99.5 0.6 fusion.23
  100.1 0.2 maximum_maximum_fusion.1.grid_ref
  100.3 0.3 multiply_add_fusion
  100.7 1.6 %pad_maximum_fusion = f32[2,32,16,512]{3,2,1,0:T(8,128)} fusion(f32[1,32,16,512]{3,2,1,0:T(8,128)S(1)} %get-tuple-element.31, f32[1,32,16,512]{3,2,1,0:T(8,128)S(1)} %get-tuple-element.30), kind=kLoop, calls=%fused_computation | loop fusion | flops 524288 | bytes 4194304 | tf_op jit(solution)/shard_map/stack | solution.py:468
  102.3 1.3 %copy-done.1 = f32[16,128,512]{2,1,0:T(8,128)S(1)} copy-done((f32[16,128,512]{2,1,0:T(8,128)S(1)}, f32[16,128,512]{2,1,0:T(8,128)}, u32[]{:S(2)}) %copy-start.1) | copy-done | bytes 4194328
  103.6 13.9 %shard_map.116 = f32[16,128,512]{2,1,0:T(8,128)} custom-call(f32[16,128,512]{2,1,0:T(8,128)S(1)} %copy-done.1, f32[16,128,512]{2,1,0:T(8,128)} %collective-permute-done.other_ref, f32[16,64,32]{2,1,0:T(8,128)S(1)} %maximum_maximum_fusion.1.grid_ref, f32[128,64]{1,0:T(8,128)S(1)} %fusion.38.tall_rows_ref, f32[32,512]{1,0:T(8,128)S(1)} %get-tuple-element.40.wide_cols_ref, ...), custom_call_target="tpu_custom_call" | custom-call | tf_op jit(solution)/shard_map/pallas_call | solution.py:270
  (50 shorter events, 0.4 us)
Async XLA Ops:
  7.2 41.6 %all-to-all-start = ((f32[16,24,128]{2,1,0:T(8,128)}), f32[16,24,128]{2,1,0:T(8,128)}, u32[]{:S(2)}, u32[]{:S(2)}) async-start(f32[16,24,128]{2,1,0:T(8,128)} %bitcast_bitcast_fusion), calls=%async_computation | async-start | bytes 393216 | tf_op jit(solution)/shard_map/all_to_all | solution.py:425
  15.6 28.1 %copy-start.7 = (s32[512]{0:T(512)}, s32[512]{0:T(512)S(1)}, u32[]{:S(2)}) copy-start(s32[512]{0:T(512)S(1)} %get-tuple-element.55) | copy-start | bytes 6148
  15.6 28.1 %copy-start.9 = (s32[512]{0:T(512)}, s32[512]{0:T(512)S(1)}, u32[]{:S(2)}) copy-start(s32[512]{0:T(512)S(1)} %get-tuple-element.56) | copy-start | bytes 6148
  16.3 27.0 %copy-start.5 = (f32[8,8]{1,0:T(8,128)}, f32[8,8]{1,0:T(8,128)S(1)}, u32[]{:S(2)}) copy-start(f32[8,8]{1,0:T(8,128)S(1)} %fusion.29) | copy-start | bytes 772
  16.7 3.4 %copy-start = (f32[32,128,512]{2,1,0:T(8,128)S(1)}, f32[32,128,512]{2,1,0:T(8,128)}, u32[]{:S(2)}) copy-start(f32[32,128,512]{2,1,0:T(8,128)} %field_ref.3) | copy-start | bytes 25165828
  20.1 23.1 %copy-start.4 = (f32[32,32]{1,0:T(8,128)S(1)}, f32[32,32]{1,0:T(8,128)}, u32[]{:S(2)}) copy-start(f32[32,32]{1,0:T(8,128)} %param.10) | copy-start | bytes 12292
  23.9 19.8 %copy-start.11 = (s32[32]{0:T(128)S(1)}, s32[32]{0:T(128)}, u32[]{:S(2)}) copy-start(s32[32]{0:T(128)} %param.12) | copy-start | bytes 388
  43.3 2.3 %copy-start.2 = (f32[32,512]{1,0:T(8,128)}, f32[32,512]{1,0:T(8,128)S(1)}, u32[]{:S(2)}) copy-start(f32[32,512]{1,0:T(8,128)S(1)} %get-tuple-element.58) | copy-start | bytes 196612
  46.5 2.3 %copy-start.13 = (s32[128]{0:T(128)S(1)}, s32[128]{0:T(128)}, u32[]{:S(2)}) copy-start(s32[128]{0:T(128)} %and_select_fusion.1) | copy-start | bytes 1540
  51.7 26.5 %copy-start.6 = (f32[8,8]{1,0:T(8,128)S(1)}, f32[8,8]{1,0:T(8,128)}, u32[]{:S(2)}) copy-start(f32[8,8]{1,0:T(8,128)} %copy-done.5) | copy-start | bytes 772
  78.0 24.2 %collective-permute-start = (f32[16,128,512]{2,1,0:T(8,128)}, f32[16,128,512]{2,1,0:T(8,128)}, u32[]{:S(2)}, u32[]{:S(2)}) collective-permute-start(f32[16,128,512]{2,1,0:T(8,128)} %get-tuple-element.7.own_ref), channel_id=1, source_target_pairs={{0,1},{1,0},{2,3},{3,2},{4,5},{5,4},{6,7},{7,6},{8,9},{9,8},{10,11... | collective-permute-start | bytes 12582920 | tf_op jit(solution)/shard_map/ppermute | solution.py:450
  78.9 17.0 %copy-start.8 = (s32[512]{0:T(512)S(1)}, s32[512]{0:T(512)}, u32[]{:S(2)}) copy-start(s32[512]{0:T(512)} %copy-done.7) | copy-start | bytes 6148
  78.9 17.1 %copy-start.10 = (s32[512]{0:T(512)S(1)}, s32[512]{0:T(512)}, u32[]{:S(2)}) copy-start(s32[512]{0:T(512)} %copy-done.9) | copy-start | bytes 6148
  78.9 17.1 %copy-start.12 = (s32[32]{0:T(128)S(1)}, s32[32]{0:T(128)}, u32[]{:S(2)}) copy-start(s32[32]{0:T(128)} %param.12) | copy-start | bytes 388
  98.0 2.3 %copy-start.3 = (f32[32,512]{1,0:T(8,128)S(1)}, f32[32,512]{1,0:T(8,128)}, u32[]{:S(2)}) copy-start(f32[32,512]{1,0:T(8,128)} %copy-done.2) | copy-start | bytes 196612
  100.6 2.9 %copy-start.1 = (f32[16,128,512]{2,1,0:T(8,128)S(1)}, f32[16,128,512]{2,1,0:T(8,128)}, u32[]{:S(2)}) copy-start(f32[16,128,512]{2,1,0:T(8,128)} %get-tuple-element.7.own_ref) | copy-start | bytes 12582916

commit v2 on v1

--- a/solution.py
+++ b/solution.py
@@ -59,9 +59,30 @@
     return mm(a[0], b[0], dims) + (mm(a[0], b[1], dims) + mm(a[1], b[0], dims))
 
 
-def pack_kernel(tiles, cap, dest_ref, vals_ref, out_ref):
-    n = dest_ref.shape[0]
-    dest = dest_ref[...]
+def stacked(x, axis):
+    hi, low = split2(x)
+    return jnp.concatenate((hi.astype(F32), low.astype(F32)), axis=axis).astype(BF16)
+
+
+def dot_tall(a_stack, b):
+    count = a_stack.shape[0] // 2
+    hi, low = split2(b)
+    both = mm(a_stack, hi)
+    return both[:count] + both[count:] + mm(a_stack[:count], low)
+
+
+def deep_left(x):
+    hi = x.astype(BF16).astype(F32)
+    return jnp.concatenate((hi, x - hi, hi), axis=1)
+
+
+def deep_right(x):
+    hi = x.astype(BF16).astype(F32)
+    return jnp.concatenate((hi, hi, x - hi), axis=0).astype(BF16)
+
+
+def pack(dest, vals, out_ref, tiles, cap):
+    n = dest.shape[0]
     wide = max(tiles, 128)
     named = dest == lax.broadcasted_iota(jnp.int32, (n, wide), 1)
     one_hot = named.astype(F32).astype(BF16)
@@ -71,7 +92,6 @@
     earlier = mm(before.astype(F32).astype(BF16), one_hot)
     rank = jnp.sum(jnp.where(named, earlier, 0.0), axis=1, keepdims=True)
     position = dest * cap + rank.astype(jnp.int32)
-    vals = vals_ref[...]
     rows = vals.shape[0]
     hi = vals.astype(BF16)
     left = vals - hi.astype(F32)
@@ -83,113 +103,93 @@
         at = lax.broadcasted_iota(jnp.int32, (n, step), 1) + first
         place = (position == at).astype(F32).astype(BF16)
         got = mm(parts, place)
-        out_ref[:, first : first + step] = (
-            got[:rows] + got[rows : 2 * rows] + got[2 * rows : 3 * rows]
-        )
-
-
-def pack_points(dest, vals, tiles, cap):
-    return pl.pallas_call(
-        functools.partial(pack_kernel, tiles, cap),
-        out_shape=jax.ShapeDtypeStruct((vals.shape[0], tiles * cap), F32),
-        compiler_params=pltpu.CompilerParams(vmem_limit_bytes=40 * MIB),
-    )(dest, vals)
-
-
-def to_modes(rows2, tall, out_ref, at, scale):
-    grid = dot3(rows2, split2(tall))
+        got = got[:rows] + got[rows : 2 * rows] + got[2 * rows : 3 * rows]
+        for at in range(0, step, cap):
+            out_ref[(first + at) // cap] = got[:, at : at + cap]
+
+
+def to_modes(rows_stack, tall, out_ref, at, scale):
+    both = mm(rows_stack, stacked(tall, 1))
+    grid = both[: 2 * A, : 2 * M] + both[2 * A :, : 2 * M] + both[: 2 * A, 2 * M :]
     out_ref[at, 0] = (grid[:A, :M] - grid[A:, M:]) * scale
     out_ref[at, 1] = (grid[A:, :M] + grid[:A, M:]) * (-scale)
-
-
-def field_modes_kernel(scale, own_ref, field_ref, cols_ref, rows_ref, out_ref):
-    count, height, width = field_ref.shape
-    cols2 = split2(cols_ref[...])
-    rows2 = split2(rows_ref[...])
-    tall = dot3(split2(field_ref[...].reshape(count * height, width)), cols2)
-    for c in range(count):
-        to_modes(rows2, tall[c * height : (c + 1) * height], out_ref, c, scale)
-
-
-def field_modes(field, own, own_count, cols, rows, scale):
-    _, height, width = field.shape
-    count = 4
-    steps = own_count // count
-    return pl.pallas_call(
-        functools.partial(field_modes_kernel, scale),
-        grid_spec=pltpu.PrefetchScalarGridSpec(
-            num_scalar_prefetch=1,
-            grid=(steps,),
-            in_specs=[
-                pl.BlockSpec((count, height, width), lambda i, own: (own[0] * steps + i, 0, 0)),
-                pl.BlockSpec(cols.shape, lambda i, own: (0, 0)),
-                pl.BlockSpec(rows.shape, lambda i, own: (0, 0)),
-            ],
-            out_specs=pl.BlockSpec((count, 2, A, M), lambda i, own: (i, 0, 0, 0)),
-        ),
-        out_shape=jax.ShapeDtypeStruct((own_count, 2, A, M), F32),
-        compiler_params=pltpu.CompilerParams(vmem_limit_bytes=40 * MIB),
-    )(own, field, cols, rows)
 
 
 def slope_kernel(
     scale, field_ref, grid_ref, tall_rows_ref, wide_cols_ref, tall_cols_ref, rows_ref, kron_ref,
     bias_ref, vals_ref, rowid_ref, colid_ref, group_ref,
     slope_ref, modes_ref, point_ref,
-    half_ref, hot_ref, vhi_ref, vlo_ref, tall_ref, acc_ref,
+    half_ref, hot_ref, v_ref, tall_ref, acc_ref, kron2_ref, wide2_ref, cols2_ref,
 ):
     step = pl.program_id(0)
-    channels, _, width = slope_ref.shape
+    channels, block, width = slope_ref.shape
     rows = channels * RB
     points = vals_ref.shape[1]
     inputs = field_ref.shape[0]
 
     @pl.when(step == 0)
     def _():
-        tall_rows = split2(tall_rows_ref[...])
+        tall_rows = deep_left(tall_rows_ref[...]).astype(BF16)
         for o in range(channels):
-            half_ref[o] = dot3(tall_rows, split2(grid_ref[o]))
+            half_ref[o] = deep_left(mm(tall_rows, deep_right(grid_ref[o])))
         vals = vals_ref[...]
         hi = vals.astype(BF16).astype(F32)
-        low = vals - hi
-        vhi_ref[...] = jnp.broadcast_to(hi[:, None, :], (channels, RB, points)).reshape(rows, points)
-        vlo_ref[...] = jnp.broadcast_to(low[:, None, :], (channels, RB, points)).reshape(rows, points)
+        both = jnp.concatenate((hi, vals - hi), axis=0)
+        both = jnp.broadcast_to(both[:, None, :], (2 * channels, RB, points))
+        v_ref[...] = both.reshape(2 * rows, points).astype(BF16)
         part = 256
         for first in range(0, points, part):
             ids = colid_ref[first : first + part, :]
             hot = ids == lax.broadcasted_iota(jnp.int32, (part, width), 1)
             hot_ref[first : first + part, :] = hot.astype(F32).astype(BF16)
         acc_ref[...] = jnp.zeros_like(acc_ref)
-
-    block2 = split2(field_ref[...].reshape(inputs * RB, width))
-    half = half_ref[:, pl.ds(pl.multiple_of(step * RB, RB), RB), :].reshape(rows, 2 * M)
-    pre = (
-        dot3(split2(half), split2(wide_cols_ref[...]))
-        + dot3(split2(kron_ref[...]), block2)
-        + bias_ref[...]
-    )
-    here = rowid_ref[...] == step * RB + lax.broadcasted_iota(jnp.int32, (RB, points), 0)
-    here = jnp.broadcast_to(here.astype(F32)[None], (channels, RB, points)).reshape(rows, points)
-    cot = mm((vhi_ref[...] * here).astype(BF16), hot_ref[...]) + mm(
-        (vlo_ref[...] * here).astype(BF16), hot_ref[...]
-    )
+        kron2_ref[...] = stacked(kron_ref[...], 0)
+        wide2_ref[...] = deep_right(wide_cols_ref[...])
+        cols2_ref[...] = stacked(tall_cols_ref[...], 1)
+
+    subs = block // RB
+    picked = []
+    for u in range(subs):
+        first = step * block + u * RB
+        here = rowid_ref[...] == first + lax.broadcasted_iota(jnp.int32, (RB, points), 0)
+        here = here.astype(F32)
+        here = jnp.concatenate((here, here), axis=0).astype(BF16)
+        here = jnp.broadcast_to(here[None], (rows // RB, 2 * RB, points)).reshape(2 * rows, points)
+        picked.append(v_ref[...] * here)
+    cots = mm(jnp.concatenate(picked, axis=0), hot_ref[...])
     k = math.sqrt(2.0 / math.pi)
-    square = pre * pre
-    t = jnp.tanh(k * pre * (1.0 + 0.044715 * square))
-    rate = 0.5 * (1.0 + t) + 0.5 * k * pre * (1.0 - t * t) * (1.0 + 3 * 0.044715 * square)
-    slope = cot * rate
-    slope_ref[...] = slope.reshape(channels, RB, width)
-    slope2 = split2(slope)
-    tall = dot3(slope2, split2(tall_cols_ref[...]))
-    tall_ref[:, pl.ds(pl.multiple_of(step * RB, RB), RB), :] = tall.reshape(channels, RB, 2 * M)
-    acc_ref[...] += dot3(block2, slope2, NT)
+    fields, slopes = [], []
+    for u in range(subs):
+        first = pl.multiple_of(step * block + u * RB, RB)
+        hi, low = split2(field_ref[:, u * RB : (u + 1) * RB, :].reshape(inputs * RB, width))
+        half = half_ref[:, pl.ds(first, RB), :].reshape(rows, 6 * M).astype(BF16)
+        both = mm(kron2_ref[...], hi)
+        pre = (
+            mm(half, wide2_ref[...])
+            + (both[:rows] + both[rows:] + mm(kron2_ref[:rows, :], low))
+            + bias_ref[...]
+        )
+        cot = cots[2 * rows * u : 2 * rows * u + rows] + cots[2 * rows * u + rows : 2 * rows * (u + 1)]
+        square = pre * pre
+        t = jnp.tanh(k * pre * (1.0 + 0.044715 * square))
+        rate = 0.5 * (1.0 + t) + 0.5 * k * pre * (1.0 - t * t) * (1.0 + 3 * 0.044715 * square)
+        slope = cot * rate
+        slope_ref[:, u * RB : (u + 1) * RB, :] = slope.reshape(channels, RB, width)
+        parts = stacked(slope, 0)
+        got = mm(parts, cols2_ref[...])
+        tall = got[:rows, : 2 * M] + got[:rows, 2 * M :] + got[rows:, : 2 * M]
+        tall_ref[:, pl.ds(first, RB), :] = tall.reshape(channels, RB, 2 * M)
+        fields.append(jnp.concatenate((hi, low), axis=0))
+        slopes.append(parts)
+    acc_ref[...] += mm(jnp.concatenate(fields, axis=1), jnp.concatenate(slopes, axis=1), NT)
 
     @pl.when(step == pl.num_programs(0) - 1)
     def _():
-        rows2 = split2(rows_ref[...])
+        rows_stack = stacked(rows_ref[...], 0)
         for o in range(channels):
-            to_modes(rows2, tall_ref[o], modes_ref, o, scale)
-        total = acc_ref[...]
+            to_modes(rows_stack, tall_ref[o], modes_ref, o, scale)
+        total = acc_ref[: inputs * RB, :] + acc_ref[inputs * RB :, :]
+        total = total[:, :rows] + total[:, rows:]
         same = lax.broadcasted_iota(jnp.int32, total.shape, 0) % RB == (
             lax.broadcasted_iota(jnp.int32, total.shape, 1) % RB
         )
@@ -215,11 +215,11 @@
     args = (field, grid, rows_t, wide_cols, cols_t, rows, kron, bias, vals, rowid, colid, group)
     return pl.pallas_call(
         functools.partial(slope_kernel, scale),
-        grid=(height // RB,),
-        in_specs=[pl.BlockSpec((inputs, RB, width), lambda i: (0, i, 0))]
+        grid=(height // (2 * RB),),
+        in_specs=[pl.BlockSpec((inputs, 2 * RB, width), lambda i: (0, i, 0))]
         + [whole(arg.shape) for arg in args[1:]],
         out_specs=[
-            pl.BlockSpec((channels, RB, width), lambda i: (0, i, 0)),
+            pl.BlockSpec((channels, 2 * RB, width), lambda i: (0, i, 0)),
             whole((channels, 2, A, M)),
             whole((inputs, channels)),
         ],
@@ -229,20 +229,22 @@
             jax.ShapeDtypeStruct((inputs, channels), F32),
         ],
         scratch_shapes=[
+            pltpu.VMEM((channels, height, 6 * M), F32),
+            pltpu.VMEM((points, width), BF16),
+            pltpu.VMEM((2 * lanes, points), BF16),
             pltpu.VMEM((channels, height, 2 * M), F32),
-            pltpu.VMEM((points, width), BF16),
-            pltpu.VMEM((lanes, points), F32),
-            pltpu.VMEM((lanes, points), F32),
-            pltpu.VMEM((channels, height, 2 * M), F32),
-            pltpu.VMEM((inputs * RB, lanes), F32),
+            pltpu.VMEM((2 * inputs * RB, 2 * lanes), F32),
+            pltpu.VMEM((2 * lanes, inputs * RB), BF16),
+            pltpu.VMEM((6 * M, width), BF16),
+            pltpu.VMEM((width, 4 * M), BF16),
         ],
         compiler_params=pltpu.CompilerParams(vmem_limit_bytes=52 * MIB),
     )(*args)
 
 
 def back_kernel(
-    own_ref, other_ref, grid_ref, tall_rows_ref, wide_cols_ref, kron_own_ref, kron_other_ref,
-    out_ref, half_ref,
+    own_ref, other_ref, grid_ref, tall_rows_ref, wide_cols_ref, kron_ref, out_ref,
+    half_ref, kron2_ref, wide2_ref,
 ):
     step = pl.program_id(0)
     channels, block, width = out_ref.shape
@@ -250,72 +252,93 @@
 
     @pl.when(step == 0)
     def _():
-        tall_rows = split2(tall_rows_ref[...])
+        tall_rows = deep_left(tall_rows_ref[...]).astype(BF16)
         for c in range(channels):
-            half_ref[c] = dot3(tall_rows, split2(grid_ref[c]))
-
-    half = half_ref[:, pl.ds(pl.multiple_of(step * RB, RB), RB), :].reshape(rows, 2 * M)
-    result = (
-        dot3(split2(half), split2(wide_cols_ref[...]))
-        + dot3(split2(kron_own_ref[...]), split2(own_ref[...].reshape(rows, width)))
-        + dot3(split2(kron_other_ref[...]), split2(other_ref[...].reshape(rows, width)))
-    )
-    out_ref[...] = result.reshape(channels, RB, width)
-
-
-def back_pass(own, other, grid, rows_t, wide_cols, kron_own, kron_other):
+            half_ref[c] = deep_left(mm(tall_rows, deep_right(grid_ref[c])))
+        kron2_ref[...] = stacked(kron_ref[...], 0)
+        wide2_ref[...] = deep_right(wide_cols_ref[...])
+
+    for u in range(block // RB):
+        at = slice(u * RB, (u + 1) * RB)
+        first = pl.multiple_of(step * block + u * RB, RB)
+        half = half_ref[:, pl.ds(first, RB), :].reshape(rows, 6 * M).astype(BF16)
+        slope = jnp.concatenate(
+            (own_ref[:, at, :].reshape(rows, width), other_ref[:, at, :].reshape(rows, width)),
+            axis=0,
+        )
+        result = mm(half, wide2_ref[...]) + dot_tall(kron2_ref[...], slope)
+        out_ref[:, at, :] = result.reshape(channels, RB, width)
+
+
+def back_pass(own, other, grid, rows_t, wide_cols, kron):
     channels, height, width = own.shape
-    args = (own, other, grid, rows_t, wide_cols, kron_own, kron_other)
-    block = pl.BlockSpec((channels, RB, width), lambda i: (0, i, 0))
+    args = (own, other, grid, rows_t, wide_cols, kron)
+    block = pl.BlockSpec((channels, 4 * RB, width), lambda i: (0, i, 0))
     return pl.pallas_call(
         back_kernel,
-        grid=(height // RB,),
+        grid=(height // (4 * RB),),
         in_specs=[block, block] + [whole(arg.shape) for arg in args[2:]],
         out_specs=block,
         out_shape=jax.ShapeDtypeStruct((channels, height, width), F32),
-        scratch_shapes=[pltpu.VMEM((channels, height, 2 * M), F32)],
+        scratch_shapes=[
+            pltpu.VMEM((channels, height, 6 * M), F32),
+            pltpu.VMEM((2 * kron.shape[0], kron.shape[1]), BF16),
+            pltpu.VMEM((6 * M, width), BF16),
+        ],
         compiler_params=pltpu.CompilerParams(vmem_limit_bytes=40 * MIB),
     )(*args)
 
 
-def sum_kernel(n_row, n_col, x_ref, out_ref, landed, total, gathered, send1, recv1, send2, recv2):
+MESH = pl.DeviceIdType.MESH
+
+
+def greet_all(n_row, n_col):
     n = n_row * n_col
-    row = lax.axis_index("row")
-    col = lax.axis_index("col")
-    ch = lax.axis_index("ch")
-    me = row * n_col + col
-
-    def device(offset, flip):
-        at = lax.rem(me + offset, n)
-        return (at // n_col, lax.rem(at, n_col), lax.rem(ch + flip, 2))
-
     barrier = pltpu.get_barrier_semaphore()
 
     def greet(i, carry):
         pl.semaphore_signal(
-            barrier, inc=1, device_id=device(i // 2, lax.rem(i, 2)),
-            device_id_type=pl.DeviceIdType.MESH,
+            barrier, inc=1, device_id=device_at(n_row, n_col, i // 2, i % 2), device_id_type=MESH
         )
         return carry
 
     lax.fori_loop(1, 2 * n, greet, 0)
-    pl.semaphore_wait(barrier, 2 * n - 1)
-
-    def scatter(k):
+    return barrier
+
+
+def device_at(n_row, n_col, offset, flip):
+    n = n_row * n_col
+    at = lax.rem(lax.axis_index("row") * n_col + lax.axis_index("col") + offset, n)
+    return (at // n_col, lax.rem(at, n_col), lax.rem(lax.axis_index("ch") + flip, 2))
+
+
+def send_slices(n_row, n_col, x_ref, landed, send, recv):
+    n = n_row * n_col
+    me = lax.axis_index("row") * n_col + lax.axis_index("col")
+
+    def copy(k):
         return pltpu.make_async_remote_copy(
             src_ref=x_ref.at[lax.rem(me + k, n)],
             dst_ref=landed.at[k],
-            send_sem=send1.at[k],
-            recv_sem=recv1.at[k],
-            device_id=device(k, 0),
-            device_id_type=pl.DeviceIdType.MESH,
-        )
-
-    def start1(k, carry):
-        scatter(k).start()
+            send_sem=send.at[k],
+            recv_sem=recv.at[k],
+            device_id=device_at(n_row, n_col, k, 0),
+            device_id_type=MESH,
+        )
+
+    def start(k, carry):
+        copy(k).start()
         return carry
 
-    lax.fori_loop(1, n, start1, 0)
+    lax.fori_loop(1, n, start, 0)
+    return copy
+
+
+def sum_all(n_row, n_col, x_ref, landed, total, gathered, send1, recv1, send2, recv2):
+    n = n_row * n_col
+    ch = lax.axis_index("ch")
+    me = lax.axis_index("row") * n_col + lax.axis_index("col")
+    scatter = send_slices(n_row, n_col, x_ref, landed, send1, recv1)
     total[...] = x_ref[me]
 
     def take(k, carry):
@@ -332,8 +355,8 @@
             dst_ref=gathered.at[ch * n + me],
             send_sem=send2.at[i],
             recv_sem=recv2.at[i],
-            device_id=device(i // 2, lax.rem(i, 2)),
-            device_id_type=pl.DeviceIdType.MESH,
+            device_id=device_at(n_row, n_col, i // 2, i % 2),
+            device_id_type=MESH,
         )
 
     def start2(i, carry):
@@ -353,7 +376,108 @@
         return carry
 
     lax.fori_loop(1, 2 * n, end2, 0)
+
+
+def sum_kernel(n_row, n_col, x_ref, out_ref, landed, total, gathered, send1, recv1, send2, recv2):
+    barrier = greet_all(n_row, n_col)
+    pl.semaphore_wait(barrier, 2 * n_row * n_col - 1)
+    sum_all(n_row, n_col, x_ref, landed, total, gathered, send1, recv1, send2, recv2)
     out_ref[...] = gathered[...]
+
+
+def front_kernel(
+    n_row, n_col, own, scale, dest_ref, vals_ref, cols_ref, rows_ref, field_ref, got_ref, out_ref,
+    held, held_sem, grouped, came, tall_ref, x_ref, landed, total, gathered,
+    send0, recv0, send1, recv1, send2, recv2,
+):
+    n = n_row * n_col
+    count, height, width = held.shape[1:]
+    cap = grouped.shape[2]
+    ch = lax.axis_index("ch")
+    me = lax.axis_index("row") * n_col + lax.axis_index("col")
+    loads = [
+        pltpu.make_async_copy(
+            field_ref.at[pl.ds(ch * own + i * count, count)], held.at[i], held_sem.at[i]
+        )
+        for i in range(own // count)
+    ]
+    for load in loads:
+        load.start()
+    barrier = greet_all(n_row, n_col)
+    pack(dest_ref[...], vals_ref[...], grouped, n, cap)
+    pl.semaphore_wait(barrier, 2 * n - 1)
+    trade = send_slices(n_row, n_col, grouped, came, send0, recv0)
+    came[0] = grouped[me]
+
+    cols2 = stacked(cols_ref[...], 1)
+    for i, load in enumerate(loads):
+        load.wait()
+        both = mm(stacked(held[i].reshape(count * height, width), 0), cols2)
+        half = count * height
+        tall = both[:half, : 2 * M] + both[:half, 2 * M :] + both[half:, : 2 * M]
+        for c in range(count):
+            at = (i * count + c) * M
+            tall_ref[:, at : at + M] = tall[c * height : (c + 1) * height, :M]
+            at = at + own * M
+            tall_ref[:, at : at + M] = tall[c * height : (c + 1) * height, M:]
+    side = own * M
+    both = mm(stacked(rows_ref[...], 0), stacked(tall_ref[...], 1))
+    grid = both[: 2 * A, : 2 * side] + both[2 * A :, : 2 * side] + both[: 2 * A, 2 * side :]
+    re = (grid[:A, :side] - grid[A:, side:]) * scale
+    im = (grid[A:, :side] + grid[:A, side:]) * (-scale)
+    lines = jnp.concatenate(
+        [part[:, at : at + 128] for part in (re, im) for at in range(0, side, 128)], axis=0
+    )
+    deep = lines.shape[0] // n
+    for p in range(n):
+        x_ref[p] = lines[p * deep : (p + 1) * deep]
+    sum_all(n_row, n_col, x_ref, landed, total, gathered, send1, recv1, send2, recv2)
+    out_ref[...] = gathered[...]
+
+    def end0(k, carry):
+        trade(k).wait()
+        return carry
+
+    lax.fori_loop(1, n, end0, 0)
+    for p in range(n):
+        got_ref[:, p * cap : (p + 1) * cap] = came[p]
+
+
+def front_pass(dest, vals, cols_t, rows, field, own, cap, scale, n_row, n_col):
+    n = n_row * n_col
+    _, height, width = field.shape
+    count = 4
+    deep = own * 2 * MODES // 128 // n
+    kept = vals.shape[0]
+    vmem = pl.BlockSpec(memory_space=pltpu.VMEM)
+    got, out = pl.pallas_call(
+        functools.partial(front_kernel, n_row, n_col, own, scale),
+        out_shape=[
+            jax.ShapeDtypeStruct((kept, n * cap), F32),
+            jax.ShapeDtypeStruct((2 * n, deep, 128), F32),
+        ],
+        in_specs=[vmem, vmem, vmem, vmem, pl.BlockSpec(memory_space=pl.ANY)],
+        out_specs=[vmem, vmem],
+        scratch_shapes=[
+            pltpu.VMEM((own // count, count, height, width), F32),
+            pltpu.SemaphoreType.DMA((own // count,)),
+            pltpu.VMEM((n, kept, cap), F32),
+            pltpu.VMEM((n, kept, cap), F32),
+            pltpu.VMEM((height, 2 * own * M), F32),
+            pltpu.VMEM((n, deep, 128), F32),
+            pltpu.VMEM((n, deep, 128), F32),
+            pltpu.VMEM((deep, 128), F32),
+            pltpu.VMEM((2 * n, deep, 128), F32),
+        ]
+        + [pltpu.SemaphoreType.DMA((n,))] * 4
+        + [pltpu.SemaphoreType.DMA((2 * n,))] * 2,
+        compiler_params=pltpu.CompilerParams(
+            collective_id=0, has_side_effects=True, vmem_limit_bytes=44 * MIB
+        ),
+    )(dest, vals, cols_t, rows, field)
+    wide = 128 // M
+    spec = out.reshape(2, 2, own // wide, A, wide, M).transpose(1, 0, 2, 4, 3, 5)
+    return got, spec.reshape(2, 2 * own, MODES)
 
 
 def device_sum(x, n_row, n_col, which):
@@ -420,17 +544,13 @@
     vals = jnp.concatenate(
         (residual, (trace_cell + 1).astype(F32)[None, :], jnp.zeros((7, points), F32)), axis=0
     )
-    packed = pack_points(trace_dest, vals, tiles, cap)
-    packed = packed.reshape(own + 8, tiles, cap).transpose(1, 0, 2)
-    got = lax.all_to_all(packed, ("row", "col"), split_axis=0, concat_axis=0, tiled=True)
-    got = got.transpose(1, 0, 2).reshape(own + 8, tiles * cap)
+    got, spec = front_pass(
+        trace_dest, vals, cols_t, rows, field, own, cap, forward_scale, n_row, n_col
+    )
+    spec_re, spec_im = spec[0], spec[1]
     cell = got[own].astype(jnp.int32) - 1
     rowid = jnp.where(cell < 0, -1, cell // width)[None, :]
     colid = jnp.where(cell < 0, -1, cell % width)[:, None]
-
-    part = field_modes(field, ch.reshape(1), own, cols_t, rows, forward_scale)
-    spec = device_sum(part.reshape(-1), n_row, n_col, 0).reshape(inputs, 2, MODES)
-    spec_re, spec_im = spec[:, 0], spec[:, 1]
 
     allowed = mode_mask(kept_modes)
     own_allowed = lax.dynamic_slice_in_dim(allowed, first, own, 0)
@@ -478,11 +598,17 @@
     adjoint_re = jnp.sum(in_w[0] * all_re[None] + in_w[1] * all_im[None], axis=1)
     adjoint_im = jnp.sum(in_w[0] * all_im[None] - in_w[1] * all_re[None], axis=1)
     own_point = lax.dynamic_slice_in_dim(point_weight, first, own, 0)
-    kron_own = spread_rows(lax.dynamic_slice_in_dim(own_point, first, own, 1))
-    kron_other = spread_rows(lax.dynamic_slice_in_dim(own_point, own - first, own, 1))
+    kron_back = spread_rows(
+        jnp.concatenate(
+            (
+                lax.dynamic_slice_in_dim(own_point, first, own, 1),
+                lax.dynamic_slice_in_dim(own_point, own - first, own, 1),
+            ),
+            axis=1,
+        )
+    )
     grad_field = back_pass(
-        slope, other_slope, mode_grid(adjoint_re, adjoint_im), rows_t, wide_cols, kron_own,
-        kron_other,
+        slope, other_slope, mode_grid(adjoint_re, adjoint_im), rows_t, wide_cols, kron_back
     )
     return (grad_field, grad_spec, grad_point, grad_bias)
 

time: 118 us -> 99.7 us (0.84)
  Pallas kernels: 78.8 us -> 69.7 us
  starting transfers between devices: 8.43 us -> 0.1 us
  local copies, waits for them, and re-layouts: 17 us -> 14.7 us
  other arithmetic: 12 us -> 13.6 us
    pallas_call x2 -> x1, Pallas kernels: 31.5 us -> 16.4 us  [device_sum(): pl.pallas_call(functools.partial(sum_kernel, n_row, n_col), out_shape=jax...]
    all_to_all x1 -> x0, starting transfers between devices: 8.37 us -> none  [per_device(): lax.all_to_all(packed, ('row', 'col'), split_axis=0, concat_axis=0, tiled...]
    pallas_call x4 -> x3, Pallas kernels: 47.4 us -> 53.3 us  [the longest x1 24.4 us: slope_pass(): pl.pallas_call(functools.partial(slope_kernel, scale), grid=(height // (2...]
    mul x2 -> x1, other arithmetic: 0.52 us -> 1.73 us  [spread_rows(): weights[:, None, :, None] * eye[None, :, None, :]]
    mul x3 -> x2, local copies, waits for them, and re-layouts: 2.21 us -> 2.43 us  [spread_rows(): weights[:, None, :, None] * eye[None, :, None, :]]
    unnamed x33 -> x19, local copies, waits for them, and re-layouts: 6.4 us -> 6.3 us
  transfers between devices with their start and end apart: 2 -> 1, of which waited for: 0 -> 0; matrix products, arithmetic and copies ran while one was open for 15% -> 11% of each run, Pallas kernels for 30% -> 17%
where the time goes in v2:
time: 99.7 us; the launch traced here: 99.2 us
  Pallas kernels  69.7 us (70%)
  local copies, waits for them, and re-layouts  14.7 us (15%)
  other arithmetic  13.6 us (14%)
  between operations  1.06 us (1%)
    pallas_call x1, Pallas kernels, slope_pass(): pl.pallas_call(functools.partial(slope_kernel, scale), grid=(height // (2...  24.4 us
    pallas_call x1, Pallas kernels, front_pass(): pl.pallas_call(functools.partial(front_kernel, n_row, n_col, own, scale),...  22 us
    pallas_call x1, Pallas kernels, device_sum(): pl.pallas_call(functools.partial(sum_kernel, n_row, n_col), out_shape=jax...  16.4 us
    pallas_call x1, Pallas kernels, back_pass(): pl.pallas_call(back_kernel, grid=(height // (4 * RB),), in_specs=[block,...  6.99 us
    unnamed x19, local copies, waits for them, and re-layouts  6.3 us
    mul x2, local copies, waits for them, and re-layouts, spread_rows(): weights[:, None, :, None] * eye[None, :, None, :]  2.43 us
    reduce_sum x1, other arithmetic, per_device(): jnp.sum(in_w[0] * all_im[None] - in_w[1] * all_re[None], axis=1)  2.12 us
  transfers between devices with their start and end apart: 1, of which 0 were waited for; matrix products, arithmetic and copies ran while one was open for 11% of the time, Pallas kernels for 17%

profile of v2, /device:TPU:0, one launch (start us, length us, event | category | flops | bytes accessed | tf_op | source)
XLA Modules:
  0.0 99.2 jit_solution(10927205673402972880)
XLA Ops:
  0.7 0.1 fusion.17
  0.8 0.1 copy.57
  0.9 0.2 multiply_cosine_fusion
  1.1 0.1 pad_maximum_fusion.3
  1.2 0.1 fusion.38.tall_rows_ref
  1.3 0.9 copy.58.dest_ref
  2.2 0.7 add_convert_fusion
  2.9 0.2 fusion.21
  3.1 0.1 copy.59.cols_ref.tall_cols_ref
  3.2 0.1 copy.60.rows_ref
  3.3 0.1 pad.27.clone
  3.4 0.9 maximum_maximum_fusion.2.vals_ref
  4.3 3.4 %copy-done = f32[32,128,512]{2,1,0:T(8,128)S(1)} copy-done((f32[32,128,512]{2,1,0:T(8,128)S(1)}, f32[32,128,512]{2,1,0:T(8,128)}, u32[]{:S(2)}) %copy-start) | copy-done | bytes 8388632
  7.7 22.0 %shard_map.111 = (f32[24,2048]{1,0:T(8,128)S(1)}, f32[32,8,128]{2,1,0:T(8,128)S(1)}) custom-call(s32[1024,1]{1,0:T(8,128)S(1)} %copy.58.dest_ref, f32[24,1024]{1,0:T(8,128)S(1)} %maximum_maximum_fusion.2.vals_ref, f32[512,32]{1,0:T(8,128)S(1)} %copy.59.cols_ref.tall_cols_ref, f32[64,128]{1,0:T(8,128)S(1)} %copy.60.rows_ref, f32[32,128,512]{2,1,0:T(8,128)S(1)} %copy-done), custom_call_target="tpu_custom_call" | custom-call | tf_op jit(solution)/shard_map/pallas_call | solution.py:453
  29.7 0.1 fusion.33
  29.8 0.3 reshape.334
  30.1 0.1 fusion.34
  30.2 0.1 copy.62
  30.3 0.3 mul.288
  30.5 0.1 copy.61
  30.7 0.3 mul.285
  30.9 0.1 compare_and_fusion
  31.0 1.9 %add_reduce_fusion.1 = (f32[16,512]{1,0:T(8,128)S(1)}, f32[16,512]{1,0:T(8,128)S(1)}) fusion(f32[2,32,32,512]{3,2,1,0:T(8,128)} %param.9, s32[]{:T(128)S(6)} %select_n.112, s32[]{:T(128)S(6)} %add.147, f32[32,512]{1,0:T(8,128)S(1)} %mul.288, f32[32,512]{1,0:T(8,128)S(1)} %mul.285), kind=kLoop, calls=%fused_computation.16 | loop fusion | flops 2080768 | bytes 2293768 | tf_op jit(solution)/shard_map/reduce_sum | solution.py:561
  32.9 0.1 reshape.335
  33.1 0.1 reshape.336
  33.2 0.7 neg.9
  33.9 0.1 dynamic-slice_bitcast_fusion.4
  34.0 0.1 copy.63
  34.1 0.1 fusion.37
  34.1 0.1 pad_maximum_fusion.4
  34.2 1.7 %broadcast_multiply_fusion = (f32[16,8,32,8]{3,2,1,0:T(8,128)}, f32[16,8,32,8]{3,2,1,0:T(8,128)S(1)}) fusion(f32[16,32]{1,0:T(8,128)S(1)} %pad_maximum_fusion.4, f32[8,8]{1,0:T(8,128)S(1)} %fusion.28, f32[16,32]{1,0:T(8,128)S(1)} %copy.63), kind=kLoop, calls=%fused_computation.12 | loop fusion | flops 65536 | bytes 266496 | tf_op jit(solution)/shard_map/mul | solution.py:519
  35.9 1.2 %mul.300.kron_ref = f32[128,256]{1,0:T(8,128)S(1)} reshape(f32[16,8,32,8]{3,2,1,0:T(8,128)S(1)} %get-tuple-element.53) | data formatting | bytes 262144 | tf_op jit(solution)/shard_map/mul | solution.py:519
  37.2 0.1 broadcast_in_dim.11
  37.2 0.1 broadcast_in_dim_reshape.4.bias_ref
  37.3 0.4 copy.64
  37.7 1.4 %compare_select_fusion.colid_ref = s32[2048,1]{1,0:T(8,128)} fusion(s32[2048,1]{1,0:T(8,128)S(1)} %copy.64), kind=kLoop, calls=%fused_computation.5 | loop fusion | flops 24576 | bytes 16384 | tf_op jit(solution)/shard_map/jit(_where)/select_n | solution.py:553
  39.1 0.1 fusion.6.group_ref
  39.2 0.2 maximum_maximum_fusion.grid_ref
  39.4 24.4 %shard_map.112 = (f32[16,128,512]{2,1,0:T(8,128)}, f32[16,2,32,16]{3,2,1,0:T(8,128)S(1)}, f32[32,16]{1,0:T(8,128)S(1)}) custom-call(f32[32,128,512]{2,1,0:T(8,128)} %field_ref.3, f32[16,64,32]{2,1,0:T(8,128)S(1)} %maximum_maximum_fusion.grid_ref, f32[128,64]{1,0:T(8,128)S(1)} %fusion.38.tall_rows_ref, f32[32,512]{1,0:T(8,128)S(1)} %get-tuple-element.42.wide_cols_ref, ...), custom_call_target="tpu_custom_call" | custom-call | tf_op jit(solution)/shard_map/pallas_call | solution.py:216
  63.8 0.1 collective-permute-start
  63.9 0.1 reshape.338
  63.9 0.2 reshape.337
  64.1 0.7 reshape.339.x_ref
  64.8 16.4 %shard_map.113 = f32[32,9,128]{2,1,0:T(8,128)} custom-call(f32[16,9,128]{2,1,0:T(8,128)} %reshape.339.x_ref), custom_call_target="tpu_custom_call" | custom-call | tf_op jit(solution)/shard_map/pallas_call | solution.py:488
  81.2 1.0 %reshape.340 = f32[2,18432]{1,0:T(2,128)S(1)} reshape(f32[32,9,128]{2,1,0:T(8,128)} %shard_map.113) | data formatting | bytes 294912 | tf_op jit(solution)/shard_map/reshape | solution.py:504
  82.3 0.7 slice.82
  82.9 0.2 reshape.341
  83.1 0.1 fusion.35
  83.2 0.1 fusion.4
  83.3 2.1 %subtract_reduce_fusion = (f32[16,512]{1,0:T(8,128)S(1)}, f32[16,512]{1,0:T(8,128)S(1)}) fusion(f32[2,32,32,512]{3,2,1,0:T(8,128)} %param.9, s32[]{:T(128)S(6)} %select_n.112, s32[]{:T(128)S(6)} %add.147, f32[32,512]{1,0:T(8,128)S(1)} %get-tuple-element.51, f32[32,512]{1,0:T(8,128)S(1)} %get-tuple-element.50), kind=kLoop, calls=%fused_computation.13 | loop fusion | flops 2080768 | bytes 2293768 | tf_op jit(solution)/shard_map/reduce_sum | solution.py:599
  85.4 0.1 reshape.342
  85.6 0.1 reshape.343
  85.7 1.2 %mul.313.kron_ref = f32[128,256]{1,0:T(8,128)S(1)} reshape(f32[16,8,32,8]{3,2,1,0:T(8,128)S(1)} %copy-done.2) | data formatting | bytes 262144 | tf_op jit(solution)/shard_map/mul | solution.py:519
  87.0 0.2 dynamic-slice_reduce_fusion
  87.2 0.1 fusion.30
  87.3 0.1 mul.328
  87.4 0.7 copy.73
  88.0 0.1 fusion.36
  88.1 0.6 fusion.23
  88.7 0.2 maximum_maximum_fusion.1.grid_ref
  89.0 0.3 multiply_add_fusion
  89.3 1.6 %pad_maximum_fusion = f32[2,32,16,512]{3,2,1,0:T(8,128)} fusion(f32[1,32,16,512]{3,2,1,0:T(8,128)S(1)} %get-tuple-element.33, f32[1,32,16,512]{3,2,1,0:T(8,128)S(1)} %get-tuple-element.32), kind=kLoop, calls=%fused_computation | loop fusion | flops 524288 | bytes 4194304 | tf_op jit(solution)/shard_map/stack | solution.py:588
  90.9 1.3 %copy-done.1 = f32[16,128,512]{2,1,0:T(8,128)S(1)} copy-done((f32[16,128,512]{2,1,0:T(8,128)S(1)}, f32[16,128,512]{2,1,0:T(8,128)}, u32[]{:S(2)}) %copy-start.1) | copy-done | bytes 4194328
  92.2 7.0 %shard_map.114 = f32[16,128,512]{2,1,0:T(8,128)} custom-call(f32[16,128,512]{2,1,0:T(8,128)S(1)} %copy-done.1, f32[16,128,512]{2,1,0:T(8,128)} %collective-permute-done.other_ref, f32[16,64,32]{2,1,0:T(8,128)S(1)} %maximum_maximum_fusion.1.grid_ref, f32[128,64]{1,0:T(8,128)S(1)} %fusion.38.tall_rows_ref, f32[32,512]{1,0:T(8,128)S(1)} %get-tuple-element.42.wide_cols_ref, ...), custom_call_target="tpu_custom_call" | custom-call | tf_op jit(solution)/shard_map/pallas_call | solution.py:277
  (31 shorter events, 0.2 us)
Async XLA Ops:
  4.3 3.4 %copy-start = (f32[32,128,512]{2,1,0:T(8,128)S(1)}, f32[32,128,512]{2,1,0:T(8,128)}, u32[]{:S(2)}) copy-start(f32[32,128,512]{2,1,0:T(8,128)} %field_ref.3) | copy-start | bytes 25165828
  30.2 0.8 copy-start.6
  30.6 3.3 %copy-start.5 = (f32[32,32]{1,0:T(8,128)S(1)}, f32[32,32]{1,0:T(8,128)}, u32[]{:S(2)}) copy-start(f32[32,32]{1,0:T(8,128)} %param.10) | copy-start | bytes 12292
  35.9 1.2 %copy-start.7 = (f32[16]{0:T(128)S(1)}, f32[16]{0:T(128)}, u32[]{:S(2)}) copy-start(f32[16]{0:T(128)} %param.11) | copy-start | bytes 196
  37.2 2.0 %copy-start.3 = (f32[16,32,16]{2,1,0:T(8,128)S(1)}, f32[16,32,16]{2,1,0:T(8,128)}, u32[]{:S(2)}) copy-start(f32[16,32,16]{2,1,0:T(8,128)} %neg.9) | copy-start | bytes 98308
  63.8 27.2 %collective-permute-start = (f32[16,128,512]{2,1,0:T(8,128)}, f32[16,128,512]{2,1,0:T(8,128)}, u32[]{:S(2)}, u32[]{:S(2)}) collective-permute-start(f32[16,128,512]{2,1,0:T(8,128)} %get-tuple-element.11.own_ref), channel_id=1, source_target_pairs={{0,1},{1,0},{2,3},{3,2},{4,5},{5,4},{6,7},{7,6},{8,9},{9,8},{10,11... | collective-permute-start | bytes 12582920 | tf_op jit(solution)/shard_map/ppermute | solution.py:570
  82.9 2.8 %copy-start.2 = (f32[16,8,32,8]{3,2,1,0:T(8,128)S(1)}, f32[16,8,32,8]{3,2,1,0:T(8,128)}, u32[]{:S(2)}) copy-start(f32[16,8,32,8]{3,2,1,0:T(8,128)} %get-tuple-element.52) | copy-start | bytes 393220
  85.4 1.5 %copy-start.4 = (f32[2,16896]{1,0:T(2,128)S(1)}, f32[2,16896]{1,0:T(2,128)}, u32[]{:S(2)}) copy-start(f32[2,16896]{1,0:T(2,128)} %slice.82) | copy-start | bytes 405508
  89.3 2.9 %copy-start.1 = (f32[16,128,512]{2,1,0:T(8,128)S(1)}, f32[16,128,512]{2,1,0:T(8,128)}, u32[]{:S(2)}) copy-start(f32[16,128,512]{2,1,0:T(8,128)} %get-tuple-element.11.own_ref) | copy-start | bytes 12582916

commit v3 on v2

--- a/solution.py
+++ b/solution.py
@@ -108,42 +108,80 @@
             out_ref[(first + at) // cap] = got[:, at : at + cap]
 
 
-def to_modes(rows_stack, tall, out_ref, at, scale):
-    both = mm(rows_stack, stacked(tall, 1))
-    grid = both[: 2 * A, : 2 * M] + both[2 * A :, : 2 * M] + both[: 2 * A, 2 * M :]
-    out_ref[at, 0] = (grid[:A, :M] - grid[A:, M:]) * scale
-    out_ref[at, 1] = (grid[A:, :M] + grid[:A, M:]) * (-scale)
+def mode_lines(rows, tall, scale):
+    side = tall.shape[1] // 2
+    both = mm(stacked(rows, 0), stacked(tall, 1))
+    grid = both[: 2 * A, : 2 * side] + both[2 * A :, : 2 * side] + both[: 2 * A, 2 * side :]
+    re = (grid[:A, :side] - grid[A:, side:]) * scale
+    im = (grid[A:, :side] + grid[:A, side:]) * (-scale)
+    return [part[:, at : at + 128] for part in (re, im) for at in range(0, side, 128)]
+
+
+def exact(a, b):
+    return lax.dot_general(
+        a, b, NN, precision=lax.Precision.HIGHEST, preferred_element_type=F32
+    )
+
+
+def iota(shape, axis):
+    return lax.broadcasted_iota(jnp.int32, shape, axis)
+
+
+def spread_rows(weights):
+    a, b = weights.shape
+    left = (iota((a * RB, a), 0) // RB == iota((a * RB, a), 1)).astype(F32)
+    right = (iota((b, b * RB), 1) // RB == iota((b, b * RB), 0)).astype(F32)
+    shape = (a * RB, b * RB)
+    same = iota(shape, 0) % RB == iota(shape, 1) % RB
+    return jnp.where(same, exact(exact(left, weights), right), 0.0)
 
 
 def slope_kernel(
-    scale, field_ref, grid_ref, tall_rows_ref, wide_cols_ref, tall_cols_ref, rows_ref, kron_ref,
-    bias_ref, vals_ref, rowid_ref, colid_ref, group_ref,
-    slope_ref, modes_ref, point_ref,
-    half_ref, hot_ref, v_ref, tall_ref, acc_ref, kron2_ref, wide2_ref, cols2_ref,
+    n_row, n_col, scale, field_ref, grid_ref, tall_rows_ref, wide_cols_ref, tall_cols_ref,
+    rows_ref, point_ref, bias_ref, got_ref,
+    slope_ref, other_ref, out_ref,
+    half_ref, hot_ref, v_ref, tall_ref, acc_ref, kron2_ref, wide2_ref, cols2_ref, rowid_ref,
+    made_ref, swap_send, swap_recv, x_ref, landed, total, gathered, send1, recv1, send2, recv2,
 ):
     step = pl.program_id(0)
+    n = n_row * n_col
     channels, block, width = slope_ref.shape
+    steps = made_ref.shape[0]
     rows = channels * RB
-    points = vals_ref.shape[1]
+    points = got_ref.shape[1]
     inputs = field_ref.shape[0]
+
+    def swap(i):
+        return pltpu.make_async_remote_copy(
+            src_ref=made_ref.at[i],
+            dst_ref=other_ref.at[:, pl.ds(i * block, block), :],
+            send_sem=swap_send.at[i],
+            recv_sem=swap_recv.at[i],
+            device_id=device_at(n_row, n_col, 0, 1),
+            device_id_type=MESH,
+        )
 
     @pl.when(step == 0)
     def _():
+        greet_all(n_row, n_col)
         tall_rows = deep_left(tall_rows_ref[...]).astype(BF16)
         for o in range(channels):
             half_ref[o] = deep_left(mm(tall_rows, deep_right(grid_ref[o])))
-        vals = vals_ref[...]
+        vals = got_ref[:channels, :]
         hi = vals.astype(BF16).astype(F32)
         both = jnp.concatenate((hi, vals - hi), axis=0)
         both = jnp.broadcast_to(both[:, None, :], (2 * channels, RB, points))
         v_ref[...] = both.reshape(2 * rows, points).astype(BF16)
-        part = 256
-        for first in range(0, points, part):
-            ids = colid_ref[first : first + part, :]
-            hot = ids == lax.broadcasted_iota(jnp.int32, (part, width), 1)
-            hot_ref[first : first + part, :] = hot.astype(F32).astype(BF16)
+        cell = got_ref[channels : channels + 1, :].astype(jnp.int32) - 1
+        rowid_ref[...] = jnp.where(cell < 0, -1, cell // width)
+        colid = jnp.where(cell < 0, -1, cell % width).astype(F32)
+        for first in range(0, points, 128):
+            ids = jnp.broadcast_to(colid[:, first : first + 128], (128, 128)).T
+            for at in range(0, width, 128):
+                hot = ids == (iota((128, 128), 1) + at).astype(F32)
+                hot_ref[first : first + 128, at : at + 128] = hot.astype(F32).astype(BF16)
         acc_ref[...] = jnp.zeros_like(acc_ref)
-        kron2_ref[...] = stacked(kron_ref[...], 0)
+        kron2_ref[...] = stacked(spread_rows(point_ref[...]), 0)
         wide2_ref[...] = deep_right(wide_cols_ref[...])
         cols2_ref[...] = stacked(tall_cols_ref[...], 1)
 
@@ -175,75 +213,118 @@
         rate = 0.5 * (1.0 + t) + 0.5 * k * pre * (1.0 - t * t) * (1.0 + 3 * 0.044715 * square)
         slope = cot * rate
         slope_ref[:, u * RB : (u + 1) * RB, :] = slope.reshape(channels, RB, width)
+        made_ref[step, :, u * RB : (u + 1) * RB, :] = slope.reshape(channels, RB, width)
         parts = stacked(slope, 0)
         got = mm(parts, cols2_ref[...])
         tall = got[:rows, : 2 * M] + got[:rows, 2 * M :] + got[rows:, : 2 * M]
-        tall_ref[:, pl.ds(first, RB), :] = tall.reshape(channels, RB, 2 * M)
+        for o in range(channels):
+            for part in range(2):
+                at = (part * channels + o) * M
+                tall_ref[pl.ds(first, RB), at : at + M] = tall[
+                    o * RB : (o + 1) * RB, part * M : (part + 1) * M
+                ]
         fields.append(jnp.concatenate((hi, low), axis=0))
         slopes.append(parts)
     acc_ref[...] += mm(jnp.concatenate(fields, axis=1), jnp.concatenate(slopes, axis=1), NT)
 
-    @pl.when(step == pl.num_programs(0) - 1)
+    @pl.when(step == 0)
     def _():
-        rows_stack = stacked(rows_ref[...], 0)
-        for o in range(channels):
-            to_modes(rows_stack, tall_ref[o], modes_ref, o, scale)
-        total = acc_ref[: inputs * RB, :] + acc_ref[inputs * RB :, :]
-        total = total[:, :rows] + total[:, rows:]
-        same = lax.broadcasted_iota(jnp.int32, total.shape, 0) % RB == (
-            lax.broadcasted_iota(jnp.int32, total.shape, 1) % RB
-        )
-        kept = jnp.sum(jnp.where(same, total, 0.0).reshape(inputs, RB, rows), axis=1)
-        point_ref[...] = lax.dot_general(
-            kept, group_ref[...], NN, precision=lax.Precision.HIGHEST, preferred_element_type=F32
-        )
+        pl.semaphore_wait(pltpu.get_barrier_semaphore(), 2 * n - 1)
+
+    swap(step).start()
+
+    @pl.when(step == steps - 1)
+    def _():
+        lines = mode_lines(rows_ref[...], tall_ref[...], scale)
+        total_point = acc_ref[: inputs * RB, :] + acc_ref[inputs * RB :, :]
+        total_point = total_point[:, :rows] + total_point[:, rows:]
+        same = iota(total_point.shape, 0) % RB == iota(total_point.shape, 1) % RB
+        kept = jnp.sum(jnp.where(same, total_point, 0.0).reshape(inputs, RB, rows), axis=1)
+        each = 128 // channels
+        group = (iota((rows, 128), 0) // RB == iota((rows, 128), 1) % channels).astype(F32)
+        wide = exact(kept, group)
+        own = iota(wide.shape, 1) // channels == iota(wide.shape, 0) % each
+        lines.append(jnp.sum(jnp.where(own, wide, 0.0).reshape(inputs // each, each, 128), axis=1))
+        deep = x_ref.shape[1]
+        count = sum(line.shape[0] for line in lines)
+        lines.append(jnp.zeros((n * deep - count, 128), F32))
+        lines = jnp.concatenate(lines, axis=0)
+        for p in range(n):
+            x_ref[p] = lines[p * deep : (p + 1) * deep]
+        sum_all(n_row, n_col, x_ref, landed, total, gathered, send1, recv1, send2, recv2)
+        out_ref[...] = gathered[...]
+
+        def end(i, carry):
+            swap(i).wait()
+            return carry
+
+        lax.fori_loop(0, steps, end, 0)
 
 
 def whole(shape):
     return pl.BlockSpec(shape, lambda i: (0,) * len(shape))
 
 
-def slope_pass(field, grid, wide_cols, cols_t, rows, rows_t, kron, bias, vals, rowid, colid, scale):
+def slope_pass(
+    field, grid, wide_cols, cols_t, rows, rows_t, point, bias, got, scale, n_row, n_col
+):
+    n = n_row * n_col
     inputs, height, width = field.shape
     channels = grid.shape[0]
-    points = vals.shape[1]
+    points = got.shape[1]
     lanes = channels * RB
-    group = (
-        jnp.arange(lanes, dtype=jnp.int32)[:, None] // RB
-        == jnp.arange(channels, dtype=jnp.int32)[None, :]
-    ).astype(F32)
-    args = (field, grid, rows_t, wide_cols, cols_t, rows, kron, bias, vals, rowid, colid, group)
-    return pl.pallas_call(
-        functools.partial(slope_kernel, scale),
-        grid=(height // (2 * RB),),
-        in_specs=[pl.BlockSpec((inputs, 2 * RB, width), lambda i: (0, i, 0))]
+    block = 2 * RB
+    steps = height // block
+    mode_count = channels * 2 * MODES // 128
+    deep = -(-(mode_count + inputs * channels // 128) // n)
+    args = (field, grid, rows_t, wide_cols, cols_t, rows, point, bias, got)
+    slope, other, out = pl.pallas_call(
+        functools.partial(slope_kernel, n_row, n_col, scale),
+        grid=(steps,),
+        in_specs=[pl.BlockSpec((inputs, block, width), lambda i: (0, i, 0))]
         + [whole(arg.shape) for arg in args[1:]],
         out_specs=[
-            pl.BlockSpec((channels, 2 * RB, width), lambda i: (0, i, 0)),
-            whole((channels, 2, A, M)),
-            whole((inputs, channels)),
+            pl.BlockSpec((channels, block, width), lambda i: (0, i, 0)),
+            pl.BlockSpec(memory_space=pl.ANY),
+            whole((2 * n, deep, 128)),
         ],
         out_shape=[
             jax.ShapeDtypeStruct((channels, height, width), F32),
-            jax.ShapeDtypeStruct((channels, 2, A, M), F32),
-            jax.ShapeDtypeStruct((inputs, channels), F32),
+            jax.ShapeDtypeStruct((channels, height, width), F32),
+            jax.ShapeDtypeStruct((2 * n, deep, 128), F32),
         ],
         scratch_shapes=[
             pltpu.VMEM((channels, height, 6 * M), F32),
             pltpu.VMEM((points, width), BF16),
             pltpu.VMEM((2 * lanes, points), BF16),
-            pltpu.VMEM((channels, height, 2 * M), F32),
+            pltpu.VMEM((height, 2 * channels * M), F32),
             pltpu.VMEM((2 * inputs * RB, 2 * lanes), F32),
             pltpu.VMEM((2 * lanes, inputs * RB), BF16),
             pltpu.VMEM((6 * M, width), BF16),
             pltpu.VMEM((width, 4 * M), BF16),
+            pltpu.VMEM((1, points), jnp.int32),
+            pltpu.VMEM((steps, channels, block, width), F32),
+            pltpu.SemaphoreType.DMA((steps,)),
+            pltpu.SemaphoreType.DMA((steps,)),
+            pltpu.VMEM((n, deep, 128), F32),
+            pltpu.VMEM((n, deep, 128), F32),
+            pltpu.VMEM((deep, 128), F32),
+            pltpu.VMEM((2 * n, deep, 128), F32),
+            pltpu.SemaphoreType.DMA((n,)),
+            pltpu.SemaphoreType.DMA((n,)),
+            pltpu.SemaphoreType.DMA((2 * n,)),
+            pltpu.SemaphoreType.DMA((2 * n,)),
         ],
-        compiler_params=pltpu.CompilerParams(vmem_limit_bytes=52 * MIB),
+        compiler_params=pltpu.CompilerParams(
+            collective_id=1, has_side_effects=True, vmem_limit_bytes=54 * MIB
+        ),
     )(*args)
+    out = out.reshape(2, n * deep, 128)
+    return slope, other, unfold(out[:, :mode_count], channels), out[:, mode_count:]
 
 
 def back_kernel(
-    own_ref, other_ref, grid_ref, tall_rows_ref, wide_cols_ref, kron_ref, out_ref,
+    own_ref, other_ref, grid_ref, tall_rows_ref, wide_cols_ref, point_ref, out_ref,
     half_ref, kron2_ref, wide2_ref,
 ):
     step = pl.program_id(0)
@@ -255,7 +336,7 @@
         tall_rows = deep_left(tall_rows_ref[...]).astype(BF16)
         for c in range(channels):
             half_ref[c] = deep_left(mm(tall_rows, deep_right(grid_ref[c])))
-        kron2_ref[...] = stacked(kron_ref[...], 0)
+        kron2_ref[...] = stacked(spread_rows(point_ref[...]), 0)
         wide2_ref[...] = deep_right(wide_cols_ref[...])
 
     for u in range(block // RB):
@@ -270,9 +351,9 @@
         out_ref[:, at, :] = result.reshape(channels, RB, width)
 
 
-def back_pass(own, other, grid, rows_t, wide_cols, kron):
+def back_pass(own, other, grid, rows_t, wide_cols, point):
     channels, height, width = own.shape
-    args = (own, other, grid, rows_t, wide_cols, kron)
+    args = (own, other, grid, rows_t, wide_cols, point)
     block = pl.BlockSpec((channels, 4 * RB, width), lambda i: (0, i, 0))
     return pl.pallas_call(
         back_kernel,
@@ -282,7 +363,7 @@
         out_shape=jax.ShapeDtypeStruct((channels, height, width), F32),
         scratch_shapes=[
             pltpu.VMEM((channels, height, 6 * M), F32),
-            pltpu.VMEM((2 * kron.shape[0], kron.shape[1]), BF16),
+            pltpu.VMEM((2 * point.shape[0] * RB, point.shape[1] * RB), BF16),
             pltpu.VMEM((6 * M, width), BF16),
         ],
         compiler_params=pltpu.CompilerParams(vmem_limit_bytes=40 * MIB),
@@ -376,13 +457,6 @@
         return carry
 
     lax.fori_loop(1, 2 * n, end2, 0)
-
-
-def sum_kernel(n_row, n_col, x_ref, out_ref, landed, total, gathered, send1, recv1, send2, recv2):
-    barrier = greet_all(n_row, n_col)
-    pl.semaphore_wait(barrier, 2 * n_row * n_col - 1)
-    sum_all(n_row, n_col, x_ref, landed, total, gathered, send1, recv1, send2, recv2)
-    out_ref[...] = gathered[...]
 
 
 def front_kernel(
@@ -420,14 +494,7 @@
             tall_ref[:, at : at + M] = tall[c * height : (c + 1) * height, :M]
             at = at + own * M
             tall_ref[:, at : at + M] = tall[c * height : (c + 1) * height, M:]
-    side = own * M
-    both = mm(stacked(rows_ref[...], 0), stacked(tall_ref[...], 1))
-    grid = both[: 2 * A, : 2 * side] + both[2 * A :, : 2 * side] + both[: 2 * A, 2 * side :]
-    re = (grid[:A, :side] - grid[A:, side:]) * scale
-    im = (grid[A:, :side] + grid[:A, side:]) * (-scale)
-    lines = jnp.concatenate(
-        [part[:, at : at + 128] for part in (re, im) for at in range(0, side, 128)], axis=0
-    )
+    lines = jnp.concatenate(mode_lines(rows_ref[...], tall_ref[...], scale), axis=0)
     deep = lines.shape[0] // n
     for p in range(n):
         x_ref[p] = lines[p * deep : (p + 1) * deep]
@@ -472,36 +539,16 @@
         + [pltpu.SemaphoreType.DMA((n,))] * 4
         + [pltpu.SemaphoreType.DMA((2 * n,))] * 2,
         compiler_params=pltpu.CompilerParams(
-            collective_id=0, has_side_effects=True, vmem_limit_bytes=44 * MIB
+            collective_id=0, has_side_effects=True, vmem_limit_bytes=58 * MIB
         ),
     )(dest, vals, cols_t, rows, field)
+    return got, unfold(out.reshape(2, n * deep, 128), own)
+
+
+def unfold(lines, own):
     wide = 128 // M
-    spec = out.reshape(2, 2, own // wide, A, wide, M).transpose(1, 0, 2, 4, 3, 5)
-    return got, spec.reshape(2, 2 * own, MODES)
-
-
-def device_sum(x, n_row, n_col, which):
-    n = n_row * n_col
-    size = x.shape[0]
-    tall = -(-size // (n * 128))
-    x = jnp.pad(x, (0, n * tall * 128 - size)).reshape(n, tall, 128)
-    out = pl.pallas_call(
-        functools.partial(sum_kernel, n_row, n_col),
-        out_shape=jax.ShapeDtypeStruct((2 * n, tall, 128), F32),
-        in_specs=[pl.BlockSpec(memory_space=pltpu.VMEM)],
-        out_specs=pl.BlockSpec(memory_space=pltpu.VMEM),
-        scratch_shapes=[
-            pltpu.VMEM((n, tall, 128), F32),
-            pltpu.VMEM((tall, 128), F32),
-            pltpu.VMEM((2 * n, tall, 128), F32),
-            pltpu.SemaphoreType.DMA((n,)),
-            pltpu.SemaphoreType.DMA((n,)),
-            pltpu.SemaphoreType.DMA((2 * n,)),
-            pltpu.SemaphoreType.DMA((2 * n,)),
-        ],
-        compiler_params=pltpu.CompilerParams(collective_id=which, has_side_effects=True),
-    )(x)
-    return out.reshape(2, n * tall * 128)[:, :size]
+    lines = lines.reshape(2, 2, own // wide, A, wide, M).transpose(1, 0, 2, 4, 3, 5)
+    return lines.reshape(2, 2 * own, MODES)
 
 
 def mode_grid(re, im):
@@ -511,12 +558,6 @@
     return jnp.concatenate(
         (jnp.concatenate((re, im), axis=2), jnp.concatenate((-im, re), axis=2)), axis=1
     )
-
-
-def spread_rows(weights):
-    eye = jnp.eye(RB, dtype=F32)
-    a, b = weights.shape
-    return (weights[:, None, :, None] * eye[None, :, None, :]).reshape(a * RB, b * RB)
 
 
 def per_device(
@@ -548,9 +589,6 @@
         trace_dest, vals, cols_t, rows, field, own, cap, forward_scale, n_row, n_col
     )
     spec_re, spec_im = spec[0], spec[1]
-    cell = got[own].astype(jnp.int32) - 1
-    rowid = jnp.where(cell < 0, -1, cell // width)[None, :]
-    colid = jnp.where(cell < 0, -1, cell % width)[:, None]
 
     allowed = mode_mask(kept_modes)
     own_allowed = lax.dynamic_slice_in_dim(allowed, first, own, 0)
@@ -561,25 +599,18 @@
     mixed_im = own_allowed * jnp.sum(
         out_w[0] * spec_im[:, None, :] + out_w[1] * spec_re[:, None, :], axis=0
     )
-    kron = spread_rows(lax.dynamic_slice_in_dim(point_weight, first, own, 1).T)
-    slope, grad_part, point_part = slope_pass(
+    out_point = lax.dynamic_slice_in_dim(point_weight, first, own, 1).T
+    slope, other_slope, modes, point_sum = slope_pass(
         field, mode_grid(mixed_re * mix_scale, mixed_im * mix_scale), wide_cols, cols_t, rows,
-        rows_t, kron, jnp.repeat(bias, RB)[:, None], got[:own], rowid, colid, mix_scale,
-    )
-    swap = [(0, 1), (1, 0)]
-    other_slope = lax.ppermute(slope, "ch", swap)
-
-    summed = device_sum(
-        jnp.concatenate((grad_part.reshape(-1), point_part.reshape(-1))), n_row, n_col, 1
-    )
-    mode_size = own * 2 * MODES
-    modes = summed[:, :mode_size].reshape(inputs, 2, MODES)
-    modes_re, modes_im = modes[:, 0], modes[:, 1]
-    mine = lax.dynamic_slice_in_dim(summed, ch, 1, 0)[0]
-    own_modes = mine[:mode_size].reshape(own, 2, MODES)
-    own_gre, own_gim = own_modes[:, 0], own_modes[:, 1]
+        rows_t, out_point, jnp.repeat(bias, RB)[:, None], got, mix_scale, n_row, n_col,
+    )
+    modes_re, modes_im = modes[0], modes[1]
+    own_modes = lax.dynamic_slice_in_dim(modes, first, own, 1)
+    own_gre, own_gim = own_modes[0], own_modes[1]
+    point_lines = inputs * own // 128
+    mine = lax.dynamic_slice_in_dim(point_sum, ch, 1, 0)[0, :point_lines]
     norm_points = 1.0 / math.sqrt(points_all)
-    grad_point = mine[mode_size:].reshape(inputs, own) * norm_points
+    grad_point = mine.reshape(inputs, own) * norm_points
     grad_bias = own_gre[:, 0] * (norm_points / mix_scale)
 
     grad_scale = math.sqrt(MODES / points_all)
@@ -598,17 +629,15 @@
     adjoint_re = jnp.sum(in_w[0] * all_re[None] + in_w[1] * all_im[None], axis=1)
     adjoint_im = jnp.sum(in_w[0] * all_im[None] - in_w[1] * all_re[None], axis=1)
     own_point = lax.dynamic_slice_in_dim(point_weight, first, own, 0)
-    kron_back = spread_rows(
-        jnp.concatenate(
-            (
-                lax.dynamic_slice_in_dim(own_point, first, own, 1),
-                lax.dynamic_slice_in_dim(own_point, own - first, own, 1),
-            ),
-            axis=1,
-        )
+    back_point = jnp.concatenate(
+        (
+            lax.dynamic_slice_in_dim(own_point, first, own, 1),
+            lax.dynamic_slice_in_dim(own_point, own - first, own, 1),
+        ),
+        axis=1,
     )
     grad_field = back_pass(
-        slope, other_slope, mode_grid(adjoint_re, adjoint_im), rows_t, wide_cols, kron_back
+        slope, other_slope, mode_grid(adjoint_re, adjoint_im), rows_t, wide_cols, back_point
     )
     return (grad_field, grad_spec, grad_point, grad_bias)
 

time: 99.7 us -> 98 us (0.983)
  Pallas kernels: 69.7 us -> 65.1 us
  local copies, waits for them, and re-layouts: 14.7 us -> 18.6 us
    pallas_call x2 -> x1, Pallas kernels: 40.8 us -> 36.1 us  [slope_pass(): pl.pallas_call(functools.partial(slope_kernel, n_row, n_col, scale), grid...]
    mul x3 -> x1, local copies, waits for them, and re-layouts: 2.51 us -> 0.08 us  [per_device(): grad_point = mine.reshape(inputs, own) * norm_points]
    mul x2 -> x1, other arithmetic: 1.83 us -> 0.01 us  [per_device(): grad_point = mine.reshape(inputs, own) * norm_points]
    pallas_call x1, Pallas kernels: 22 us -> 23.4 us  [front_pass(): pl.pallas_call(functools.partial(front_kernel, n_row, n_col, own, scale),...]
    select_n x2 -> x0, other arithmetic: 1.39 us -> none  [the longest x1 1.39 us: per_device(): colid = jnp.where(cell < 0, -1, cell % width)[:, None]]
    pallas_call x1, Pallas kernels: 6.99 us -> 5.61 us  [back_pass(): pl.pallas_call(back_kernel, grid=(height // (4 * RB),), in_specs=[block,...]
    another operation x0 -> x1, local copies, waits for them, and re-layouts: none -> 1.21 us  [unfold(): lines.reshape(2, 2, own // wide, A, wide, M).transpose(1, 0, 2, 4, 3, 5)]
    unnamed x19 -> x13, local copies, waits for them, and re-layouts: 6.3 us -> 7.44 us
  transfers between devices with their start and end apart: 1 -> 0, of which waited for: 0 -> 0; matrix products, arithmetic and copies ran while one was open for 11% -> 0% of each run, Pallas kernels for 17% -> 0%
where the time goes in v3:
time: 98 us; the launch traced here: 97.5 us
  Pallas kernels  65.1 us (66%)
  local copies, waits for them, and re-layouts  18.6 us (19%)
  other arithmetic  12.7 us (13%)
    pallas_call x1, Pallas kernels, slope_pass(): pl.pallas_call(functools.partial(slope_kernel, n_row, n_col, scale), grid...  36.1 us
    pallas_call x1, Pallas kernels, front_pass(): pl.pallas_call(functools.partial(front_kernel, n_row, n_col, own, scale),...  23.4 us
    unnamed x13, local copies, waits for them, and re-layouts  7.44 us
    pallas_call x1, Pallas kernels, back_pass(): pl.pallas_call(back_kernel, grid=(height // (4 * RB),), in_specs=[block,...  5.61 us

profile of v3, /device:TPU:0, one launch (start us, length us, event | category | flops | bytes accessed | tf_op | source)
XLA Modules:
  0.0 97.5 jit_solution(6106504751555022200)
XLA Ops:
  0.7 0.1 pad.20.clone
  0.7 0.7 add_convert_fusion
  1.4 0.7 broadcast_in_dim.8
  2.2 0.1 fusion.11
  2.3 0.9 fusion.27
  3.1 0.1 pad_maximum_fusion.4.point_ref
  3.2 0.7 compare_and_fusion
  3.9 0.8 constant_dynamic-slice_fusion.1
  4.7 0.7 copy.69
  5.4 0.1 copy.54
  5.5 0.7 broadcast_in_dim_reshape.4.bias_ref
  6.2 0.2 multiply_cosine_fusion
  6.5 0.7 fusion.28.tall_rows_ref
  7.2 0.1 pad_maximum_fusion.3
  7.3 0.7 copy.57.rows_ref
  7.9 1.5 %maximum_maximum_fusion.2.vals_ref = f32[24,1024]{1,0:T(8,128)} fusion(f32[1,1024]{1,0:T(1,128)S(1)} %bitcast.56, f32[16,1024]{1,0:T(8,128)} %param.13, f32[24]{0:T(128)S(1)} %pad.20.clone), kind=kLoop, calls=%fused_computation.13 | loop fusion | flops 49152 | bytes 168032 | tf_op jit(solution)/shard_map/concatenate | solution.py:585
  9.5 0.1 fusion.15
  9.6 0.6 pad_maximum_fusion.1
  10.3 0.8 copy.56.cols_ref.tall_cols_ref
  11.1 1.7 %copy.55.dest_ref = s32[1024,1]{1,0:T(8,128)} copy(s32[1024,1]{0,1:T(1,128)} %param.14) | data formatting | bytes 8192 | tf_op args[6]
  12.8 23.4 %shard_map.111 = (f32[24,2048]{1,0:T(8,128)}, f32[32,8,128]{2,1,0:T(8,128)}) custom-call(s32[1024,1]{1,0:T(8,128)} %copy.55.dest_ref, f32[24,1024]{1,0:T(8,128)} %maximum_maximum_fusion.2.vals_ref, f32[512,32]{1,0:T(8,128)} %copy.56.cols_ref.tall_cols_ref, f32[64,128]{1,0:T(8,128)} %copy.57.rows_ref, f32[32,128,512]{2,1,0:T(8,128)} %field_ref.3), custom_call_target="tpu_custom_call" | custom-call | tf_op jit(solution)/shard_map/pallas_call | solution.py:520
  36.2 1.2 %reshape_reshape.3 = f32[2,2,2,32,8,16]{5,4,3,2,1,0:T(8,128)S(1)} reshape(f32[32,8,128]{2,1,0:T(8,128)} %get-tuple-element.9) | data formatting | bytes 262144 | tf_op jit(solution)/shard_map/reshape;reshape | solution.py:550
  37.4 0.1 fusion.25
  37.5 0.1 copy.58
  37.6 0.3 mul.251
  37.9 0.1 copy.59
  38.0 0.3 mul.254
  38.2 1.9 %add_reduce_fusion.1 = (f32[16,512]{1,0:T(8,128)S(1)}, f32[16,512]{1,0:T(8,128)S(1)}) fusion(f32[2,32,32,512]{3,2,1,0:T(8,128)} %param.9, s32[]{:T(128)S(6)} %select_n.69, s32[]{:T(128)S(6)} %add.110, f32[32,512]{1,0:T(8,128)S(1)} %mul.254, f32[32,512]{1,0:T(8,128)S(1)} %mul.251), kind=kLoop, calls=%fused_computation.9 | loop fusion | flops 2080768 | bytes 2293768 | tf_op jit(solution)/shard_map/reduce_sum | solution.py:599
  40.2 0.1 reshape.214
  40.4 0.1 reshape.213
  40.5 1.0 %maximum_maximum_fusion.grid_ref = f32[16,64,32]{2,1,0:T(8,128)} fusion(f32[16,32,16]{2,1,0:T(8,128)S(1)} %reshape.213, f32[16,32,16]{2,1,0:T(8,128)S(1)} %neg.9, f32[16,32,16]{2,1,0:T(8,128)S(1)} %reshape.214), kind=kLoop, calls=%fused_computation.11 | loop fusion | flops 98304 | bytes 229376 | tf_op jit(solution)/shard_map/concatenate | solution.py:558
  41.5 36.1 %shard_map.112 = (f32[16,128,512]{2,1,0:T(8,128)}, f32[16,128,512]{2,1,0:T(8,128)}, f32[32,9,128]{2,1,0:T(8,128)}) custom-call(f32[32,128,512]{2,1,0:T(8,128)} %field_ref.3, f32[16,64,32]{2,1,0:T(8,128)} %maximum_maximum_fusion.grid_ref, f32[128,64]{1,0:T(8,128)} %fusion.28.tall_rows_ref, f32[32,512]{1,0:T(8,128)} %get-tuple-element.40.wide_cols_ref, ...), custom_call_target="tpu_custom_call" | custom-call | tf_op jit(solution)/shard_map/pallas_call | solution.py:281
  77.6 0.0 copy-start.4
  77.7 1.0 reshape.215
  78.7 0.1 copy.64
  78.8 0.1 mul.287
  78.9 0.7 copy.68
  79.5 0.4 reshape.216
  80.0 0.0 copy-start.2
  80.0 0.0 copy-start.3
  80.0 0.3 fusion.26
  80.3 0.2 copy.65
  80.5 0.3 squeeze.32
  80.8 0.2 copy.66
  81.0 0.3 squeeze.34
  81.3 0.0 copy-done.4
  81.3 0.1 select_multiply_fusion.1
  81.4 2.0 %subtract_reduce_fusion = (f32[16,512]{1,0:T(8,128)S(1)}, f32[16,512]{1,0:T(8,128)S(1)}) fusion(f32[2,32,32,512]{3,2,1,0:T(8,128)} %param.9, s32[]{:T(128)S(6)} %select_n.69, s32[]{:T(128)S(6)} %add.110, f32[32,512]{1,0:T(8,128)S(1)} %get-tuple-element.47, f32[32,512]{1,0:T(8,128)S(1)} %get-tuple-element.46), kind=kLoop, calls=%fused_computation.7 | loop fusion | flops 2080768 | bytes 2293768 | tf_op jit(solution)/shard_map/reduce_sum | solution.py:630
  83.4 0.1 reshape.218
  83.5 0.1 reshape.217
  83.6 0.2 maximum_maximum_fusion.1.grid_ref
  83.9 0.0 copy-done.2
  83.9 0.0 copy-done.3
  83.9 0.0 copy-start
  83.9 2.2 %copy-done = f32[16,128,512]{2,1,0:T(8,128)S(1)} copy-done((f32[16,128,512]{2,1,0:T(8,128)S(1)}, f32[16,128,512]{2,1,0:T(8,128)}, u32[]{:S(2)}) %copy-start) | copy-done | bytes 4194328
  86.1 0.0 copy-start.1
  86.1 2.2 %copy-done.1 = f32[16,128,512]{2,1,0:T(8,128)S(1)} copy-done((f32[16,128,512]{2,1,0:T(8,128)S(1)}, f32[16,128,512]{2,1,0:T(8,128)}, u32[]{:S(2)}) %copy-start.1) | copy-done | bytes 4194328
  88.3 5.6 %shard_map.113 = f32[16,128,512]{2,1,0:T(8,128)} custom-call(f32[16,128,512]{2,1,0:T(8,128)S(1)} %copy-done, f32[16,128,512]{2,1,0:T(8,128)S(1)} %copy-done.1, f32[16,64,32]{2,1,0:T(8,128)S(1)} %maximum_maximum_fusion.1.grid_ref, f32[128,64]{1,0:T(8,128)S(1)} %copy-done.2, f32[32,512]{1,0:T(8,128)S(1)} %copy-done.3, f32[16,32]{1,0:T(8,128)S(1)} %pad_maximum_fusion.4.point_ref), custom_call_target="tpu_custom_call" | custom-call | tf_op jit(solution)/shard_map/pallas_call | solution.py:358
  93.9 0.4 copy.67
  94.3 0.6 reshape.219
  94.9 0.6 fusion.16
  95.6 0.3 multiply_add_fusion
  95.9 1.6 %pad_maximum_fusion = f32[2,32,16,512]{3,2,1,0:T(8,128)} fusion(f32[1,32,16,512]{3,2,1,0:T(8,128)S(1)} %get-tuple-element.35, f32[1,32,16,512]{3,2,1,0:T(8,128)S(1)} %get-tuple-element.34), kind=kLoop, calls=%fused_computation | loop fusion | flops 524288 | bytes 4194304 | tf_op jit(solution)/shard_map/stack | solution.py:619
  (13 shorter events, 0.1 us)
Async XLA Ops:
  77.6 3.7 %copy-start.4 = (s32[32]{0:T(128)S(1)}, s32[32]{0:T(128)}, u32[]{:S(2)}) copy-start(s32[32]{0:T(128)} %param.12) | copy-start | bytes 388
  80.0 3.9 %copy-start.2 = (f32[128,64]{1,0:T(8,128)S(1)}, f32[128,64]{1,0:T(8,128)}, u32[]{:S(2)}) copy-start(f32[128,64]{1,0:T(8,128)} %fusion.28.tall_rows_ref) | copy-start | bytes 98308
  80.0 3.9 %copy-start.3 = (f32[32,512]{1,0:T(8,128)S(1)}, f32[32,512]{1,0:T(8,128)}, u32[]{:S(2)}) copy-start(f32[32,512]{1,0:T(8,128)} %get-tuple-element.40.wide_cols_ref) | copy-start | bytes 196612
  83.9 2.2 %copy-start = (f32[16,128,512]{2,1,0:T(8,128)S(1)}, f32[16,128,512]{2,1,0:T(8,128)}, u32[]{:S(2)}) copy-start(f32[16,128,512]{2,1,0:T(8,128)} %get-tuple-element.11.own_ref) | copy-start | bytes 12582916
  86.1 2.2 %copy-start.1 = (f32[16,128,512]{2,1,0:T(8,128)S(1)}, f32[16,128,512]{2,1,0:T(8,128)}, u32[]{:S(2)}) copy-start(f32[16,128,512]{2,1,0:T(8,128)} %get-tuple-element.12.other_ref) | copy-start | bytes 12582916

commit v4 on v3

--- a/solution.py
+++ b/solution.py
@@ -316,7 +316,7 @@
             pltpu.SemaphoreType.DMA((2 * n,)),
         ],
         compiler_params=pltpu.CompilerParams(
-            collective_id=1, has_side_effects=True, vmem_limit_bytes=54 * MIB
+            collective_id=1, has_side_effects=True, vmem_limit_bytes=52 * MIB
         ),
     )(*args)
     out = out.reshape(2, n * deep, 128)
@@ -366,7 +366,7 @@
             pltpu.VMEM((2 * point.shape[0] * RB, point.shape[1] * RB), BF16),
             pltpu.VMEM((6 * M, width), BF16),
         ],
-        compiler_params=pltpu.CompilerParams(vmem_limit_bytes=40 * MIB),
+        compiler_params=pltpu.CompilerParams(vmem_limit_bytes=52 * MIB),
     )(*args)
 
 
@@ -539,7 +539,7 @@
         + [pltpu.SemaphoreType.DMA((n,))] * 4
         + [pltpu.SemaphoreType.DMA((2 * n,))] * 2,
         compiler_params=pltpu.CompilerParams(
-            collective_id=0, has_side_effects=True, vmem_limit_bytes=58 * MIB
+            collective_id=0, has_side_effects=True, vmem_limit_bytes=52 * MIB
         ),
     )(dest, vals, cols_t, rows, field)
     return got, unfold(out.reshape(2, n * deep, 128), own)

time: 98 us -> 85.7 us (0.87)
  local copies, waits for them, and re-layouts: 18.6 us -> 9.03 us
  other arithmetic: 12.7 us -> 10.1 us
    unnamed x13 -> x5, local copies, waits for them, and re-layouts: 7.44 us -> 1.66 us
    pallas_call x1, Pallas kernels: 5.61 us -> 8.1 us  [back_pass(): pl.pallas_call(back_kernel, grid=(height // (4 * RB),), in_specs=[block,...]
    pallas_call x1, Pallas kernels: 23.4 us -> 21.7 us  [front_pass(): pl.pallas_call(functools.partial(front_kernel, n_row, n_col, own, scale),...]
where the time goes in v4:
time: 85.7 us; the launch traced here: 85.2 us
  Pallas kernels  65.1 us (76%)
  other arithmetic  10.1 us (12%)
  local copies, waits for them, and re-layouts  9.03 us (11%)
  between operations  0.96 us (1%)
    pallas_call x1, Pallas kernels, slope_pass(): pl.pallas_call(functools.partial(slope_kernel, n_row, n_col, scale), grid...  35.3 us
    pallas_call x1, Pallas kernels, front_pass(): pl.pallas_call(functools.partial(front_kernel, n_row, n_col, own, scale),...  21.7 us
    pallas_call x1, Pallas kernels, back_pass(): pl.pallas_call(back_kernel, grid=(height // (4 * RB),), in_specs=[block,...  8.1 us
    reduce_sum x1, other arithmetic, per_device(): jnp.sum(in_w[0] * all_im[None] - in_w[1] * all_re[None], axis=1)  1.95 us
    reduce_sum x1, other arithmetic, per_device(): jnp.sum(out_w[0] * spec_im[:, None, :] + out_w[1] * spec_re[:, None, :],...  1.95 us

profile of v4, /device:TPU:0, one launch (start us, length us, event | category | flops | bytes accessed | tf_op | source)
XLA Modules:
  0.0 85.2 jit_solution(2946179335884059717)
XLA Ops:
  0.7 0.1 pad.20.clone
  0.7 0.7 add_convert_fusion
  1.4 0.7 broadcast_in_dim.8
  2.2 0.1 fusion.11
  2.3 0.9 %fusion.27 = (f32[16,16]{1,0:T(8,128)S(1)}, f32[16,16]{1,0:T(8,128)S(1)}) fusion(f32[32,32]{1,0:T(8,128)} %param.10, s32[]{:T(128)S(6)} %select_n.73, s32[]{:T(128)S(6)} %select_n.75), kind=kLoop, calls=%fused_computation.76 | loop fusion | bytes 4104 | tf_op jit(solution)/shard_map/dynamic_slice | solution.py:634
  3.1 0.1 pad_maximum_fusion.4.point_ref
  3.2 0.7 compare_and_fusion
  3.9 0.8 constant_dynamic-slice_fusion.1
  4.7 0.1 copy.69
  4.8 0.1 copy.54
  4.9 0.1 broadcast_in_dim_reshape.4.bias_ref
  5.0 0.2 multiply_cosine_fusion
  5.2 0.1 fusion.28.tall_rows_ref
  5.3 0.1 pad_maximum_fusion.3
  5.4 0.1 copy.57.rows_ref
  5.5 0.9 %maximum_maximum_fusion.2.vals_ref = f32[24,1024]{1,0:T(8,128)S(1)} fusion(f32[1,1024]{1,0:T(1,128)S(1)} %bitcast.56, f32[16,1024]{1,0:T(8,128)} %param.13, f32[24]{0:T(128)S(1)} %pad.20.clone), kind=kLoop, calls=%fused_computation.13 | loop fusion | flops 49152 | bytes 168032 | tf_op jit(solution)/shard_map/concatenate | solution.py:585
  6.4 0.1 fusion.15
  6.6 0.1 copy.56.cols_ref.tall_cols_ref
  6.7 0.9 %copy.55.dest_ref = s32[1024,1]{1,0:T(8,128)S(1)} copy(s32[1024,1]{0,1:T(1,128)} %param.14) | data formatting | bytes 8192 | tf_op args[6]
  7.6 21.7 %shard_map.111 = (f32[24,2048]{1,0:T(8,128)S(1)}, f32[32,8,128]{2,1,0:T(8,128)S(1)}) custom-call(s32[1024,1]{1,0:T(8,128)S(1)} %copy.55.dest_ref, f32[24,1024]{1,0:T(8,128)S(1)} %maximum_maximum_fusion.2.vals_ref, f32[512,32]{1,0:T(8,128)S(1)} %copy.56.cols_ref.tall_cols_ref, f32[64,128]{1,0:T(8,128)S(1)} %copy.57.rows_ref, f32[32,128,512]{2,1,0:T(8,128)} %field_ref.3), custom_call_target="tpu_custom_call" | custom-call | tf_op jit(solution)/shard_map/pallas_call | solution.py:520
  29.4 0.3 reshape_reshape.3
  29.7 0.1 fusion.25
  29.8 0.1 copy.58
  29.9 0.3 mul.251
  30.1 0.1 copy.59
  30.2 0.3 mul.254
  30.5 1.9 %add_reduce_fusion.1 = (f32[16,512]{1,0:T(8,128)S(1)}, f32[16,512]{1,0:T(8,128)S(1)}) fusion(f32[2,32,32,512]{3,2,1,0:T(8,128)} %param.9, s32[]{:T(128)S(6)} %select_n.69, s32[]{:T(128)S(6)} %add.110, f32[32,512]{1,0:T(8,128)S(1)} %mul.254, f32[32,512]{1,0:T(8,128)S(1)} %mul.251), kind=kLoop, calls=%fused_computation.9 | loop fusion | flops 2080768 | bytes 2293768 | tf_op jit(solution)/shard_map/reduce_sum | solution.py:599
  32.5 0.1 reshape.214
  32.6 0.1 reshape.213
  32.8 0.2 maximum_maximum_fusion.grid_ref
  33.0 35.3 %shard_map.112 = (f32[16,128,512]{2,1,0:T(8,128)}, f32[16,128,512]{2,1,0:T(8,128)}, f32[32,9,128]{2,1,0:T(8,128)S(1)}) custom-call(f32[32,128,512]{2,1,0:T(8,128)} %field_ref.3, f32[16,64,32]{2,1,0:T(8,128)S(1)} %maximum_maximum_fusion.grid_ref, f32[128,64]{1,0:T(8,128)S(1)} %fusion.28.tall_rows_ref, f32[32,512]{1,0:T(8,128)S(1)} %get-tuple-element.40.wide_cols_ref, ...), custom_call_target="tpu_custom_call" | custom-call | tf_op jit(solution)/shard_map/pallas_call | solution.py:281
  68.2 0.0 copy-start
  68.3 0.1 copy.64
  68.4 0.1 mul.287
  68.5 0.7 copy.68
  69.2 0.4 reshape.216
  69.6 0.3 fusion.26
  69.9 0.2 copy.65
  70.2 0.3 squeeze.32
  70.4 0.2 copy.66
  70.7 0.3 squeeze.34
  70.9 0.0 copy-done
  70.9 0.1 select_multiply_fusion.1
  71.0 2.0 %subtract_reduce_fusion = (f32[16,512]{1,0:T(8,128)S(1)}, f32[16,512]{1,0:T(8,128)S(1)}) fusion(f32[2,32,32,512]{3,2,1,0:T(8,128)} %param.9, s32[]{:T(128)S(6)} %select_n.69, s32[]{:T(128)S(6)} %add.110, f32[32,512]{1,0:T(8,128)S(1)} %get-tuple-element.47, f32[32,512]{1,0:T(8,128)S(1)} %get-tuple-element.46), kind=kLoop, calls=%fused_computation.7 | loop fusion | flops 2080768 | bytes 2293768 | tf_op jit(solution)/shard_map/reduce_sum | solution.py:630
  73.0 0.1 reshape.218
  73.1 0.1 reshape.217
  73.3 0.2 maximum_maximum_fusion.1.grid_ref
  73.5 8.1 %shard_map.113 = f32[16,128,512]{2,1,0:T(8,128)} custom-call(f32[16,128,512]{2,1,0:T(8,128)} %get-tuple-element.11.own_ref, f32[16,128,512]{2,1,0:T(8,128)} %get-tuple-element.12.other_ref, f32[16,64,32]{2,1,0:T(8,128)S(1)} %maximum_maximum_fusion.1.grid_ref, f32[128,64]{1,0:T(8,128)S(1)} %fusion.28.tall_rows_ref, ...), custom_call_target="tpu_custom_call" | custom-call | tf_op jit(solution)/shard_map/pallas_call | solution.py:358
  81.6 0.4 copy.67
  82.0 0.6 reshape.219
  82.7 0.6 fusion.16
  83.3 0.3 multiply_add_fusion
  83.6 1.6 %pad_maximum_fusion = f32[2,32,16,512]{3,2,1,0:T(8,128)} fusion(f32[1,32,16,512]{3,2,1,0:T(8,128)S(1)} %get-tuple-element.35, f32[1,32,16,512]{3,2,1,0:T(8,128)S(1)} %get-tuple-element.34), kind=kLoop, calls=%fused_computation | loop fusion | flops 524288 | bytes 4194304 | tf_op jit(solution)/shard_map/stack | solution.py:619
  (15 shorter events, 0.2 us)
Async XLA Ops:
  68.2 2.7 %copy-start = (s32[32]{0:T(128)S(1)}, s32[32]{0:T(128)}, u32[]{:S(2)}) copy-start(s32[32]{0:T(128)} %param.12) | copy-start | bytes 388
